TPU v7x, 32 devices: a whole 2x2x4 slice. The times are simulated.
32 devices in a mesh: leaf: 4 (over y, core), front: 8 (over z, x).
Axes of the slice: x: 2, y: 2, z: 4, core: 2. Of those that a mesh axis runs over, the one named last changes fastest.
Arguments:
- leaf_inverse: bfloat16 [1024, 128, 128], P(('leaf', 'front')), may hold values from -0.5 to 0.5
- leaf_rhs: bfloat16 [1024, 128, 256], P(('leaf', 'front')), may hold values from -6 to 6
- off_blocks: bfloat16 [1024, 5, 128, 128], P(('leaf', 'front')), may hold values from -0.0546875 to 0.0546875
- block_rows: int32 [1024, 5], P(('leaf', 'front')), may hold values from 0 to 15
- fill_count: int32 [1024], P(('leaf', 'front')), may hold values from 1 to 5
- sep_rhs: bfloat16 [32, 128, 256], P(('leaf', 'front')), may hold values from -6 to 6
- panel_order: int32 [4, 8], P('leaf'), may hold values from 0 to 7, each once within a row
- sep_inverse: bfloat16 [32, 128, 1024], P(('leaf', 'front')), may hold values from -0.1875 to 0.1875
Outputs:
- leaf_solution: bfloat16 [1024, 128, 256], P(('leaf', 'front'))
- sep_forward: bfloat16 [32, 128, 256], P(('leaf', 'front'))
- sep_solution: float32 [32, 128, 256], P(('leaf', 'front'))
Inputs may be any that keep to these rules, and one draw needn't show every extreme that they name: Each row of panel_order is a permutation of the 8 separators of that front.
All inputs are finite; a program needn't handle non-finite values.
Results may differ from a plain program's by a relative error of at most 0.025.
Values may be sent and summed in bfloat16 or wider, within the bound.
A program may use at most 128 MiB of HBM per device.

v0:
```python
import jax
import jax.numpy as jnp
from jax import lax
from jax.sharding import PartitionSpec as P


def swapped(shard, axis, bit):
    return lax.ppermute(shard, axis, [(i, i ^ 1 << bit) for i in range(lax.axis_size(axis))])


def on_device(
    leaf_inverse, leaf_rhs, off_blocks, block_rows, fill_count, sep_rhs, panel_order, sep_inverse
):
    block_width = leaf_inverse.shape[1]
    probe_count = leaf_rhs.shape[2]
    owned_count = sep_rhs.shape[0]
    fronts = lax.axis_size("front")
    front_seps = owned_count * fronts
    parity = lax.axis_index("leaf") % 2
    forward = jnp.einsum(
        "kab,kbr->kar", leaf_inverse, leaf_rhs, preferred_element_type=jnp.float32
    ).astype(jnp.bfloat16)
    used_slots = jnp.arange(off_blocks.shape[1], dtype=jnp.int32)[None, :] < fill_count[:, None]
    product = jnp.einsum("kpab,kbr->kpar", off_blocks, forward, preferred_element_type=jnp.float32)
    product = jnp.where(used_slots[:, :, None, None], product, jnp.zeros((), jnp.float32))
    product = product.reshape(-1, block_width, probe_count)
    half_index = block_rows // front_seps
    local_index = block_rows % front_seps
    sibling_flag = (half_index != parity).astype(jnp.int32)
    target = (
        local_index // owned_count * (2 * owned_count)
        + sibling_flag * owned_count
        + local_index % owned_count
    )
    partial_terms = (
        jnp.zeros((2 * front_seps, block_width, probe_count), jnp.float32)
        .at[target.reshape(-1)]
        .add(product)
    )
    shares = lax.psum_scatter(
        partial_terms.astype(jnp.bfloat16), "front", scatter_dimension=0, tiled=True
    ).astype(jnp.float32)
    received = swapped(shares[owned_count:].astype(jnp.bfloat16), "leaf", 0).astype(jnp.float32)
    summed = shares[:owned_count] + received
    separator_in = (sep_rhs.astype(jnp.float32) - summed).astype(jnp.bfloat16)
    arrived = lax.all_gather(separator_in, "front", axis=0, tiled=True)
    arrived_rows = arrived.shape[0]
    columns = sep_inverse
    flat = arrived.reshape(arrived_rows * block_width, probe_count)
    forward_sep = jnp.einsum(
        "sac,cr->sar", columns, flat, preferred_element_type=jnp.float32
    ).astype(jnp.bfloat16)
    owned_rows = lax.dynamic_slice_in_dim(
        panel_order[0], lax.axis_index("front") * owned_count, owned_count
    )
    placed = (
        jnp.zeros((front_seps, block_width, probe_count), jnp.float32)
        .at[owned_rows]
        .set(forward_sep.astype(jnp.float32))
    )
    sep_forward = lax.psum_scatter(
        placed.astype(jnp.bfloat16), "front", scatter_dimension=0, tiled=True
    )
    columns = sep_inverse
    result = jnp.einsum("sac,sar->cr", columns, forward_sep, preferred_element_type=jnp.float32)
    sep_solution = lax.psum_scatter(
        result.reshape(owned_count * lax.axis_size("front"), block_width, probe_count).astype(
            jnp.bfloat16
        ),
        "front",
        scatter_dimension=0,
        tiled=True,
    ).astype(jnp.float32)
    solved = sep_solution.astype(jnp.bfloat16)
    whole_front = lax.all_gather(solved, "front", axis=0, tiled=True)
    other_front = swapped(whole_front, "leaf", 0)
    lower_front = jnp.where(parity == 0, whole_front, other_front)
    upper_front = jnp.where(parity == 0, other_front, whole_front)
    pair_field = jnp.concatenate([lower_front, upper_front], axis=0)
    picked = pair_field[block_rows]
    picked = jnp.where(used_slots[:, :, None, None], picked, jnp.zeros((), jnp.bfloat16))
    pulled = jnp.einsum("kpab,kpar->kbr", off_blocks, picked, preferred_element_type=jnp.float32)
    backward = (forward.astype(jnp.float32) - pulled).astype(jnp.bfloat16)
    leaf_solution = jnp.einsum(
        "kba,kbr->kar", leaf_inverse, backward, preferred_element_type=jnp.float32
    ).astype(jnp.bfloat16)
    return (leaf_solution, sep_forward, sep_solution)


def solution(mesh):
    placed = (
        P(("leaf", "front"), None, None),
        P(("leaf", "front"), None, None),
        P(("leaf", "front"), None, None, None),
        P(("leaf", "front"), None),
        P(("leaf", "front")),
        P(("leaf", "front"), None, None),
        P("leaf", None),
        P(("leaf", "front"), None, None),
    )
    return jax.shard_map(
        on_device,
        mesh=mesh,
        in_specs=placed,
        out_specs=(
            P(("leaf", "front"), None, None),
            P(("leaf", "front"), None, None),
            P(("leaf", "front"), None, None),
        ),
        check_vma=False,
    )
```

profile of v0, /device:TPU:0, one launch (start us, length us, event | category | flops | bytes accessed | tf_op | source)
XLA Modules:
  0.0 339.0 jit_solution(10162209435510514667)
XLA Ops:
  7.2 0.0 copy-start
  7.2 0.0 reduce-scatter.4.cloned.1.call-start
  7.2 0.8 add_select_fusion
  8.1 0.1 copy.27
  8.2 0.1 reshape.113
  8.3 0.0 copy-start.3
  8.3 0.9 iota_compare_fusion
  9.2 0.0 copy-done
  9.2 2.1 convolution_convert_fusion
  11.3 0.0 copy-done.3
  11.3 0.0 copy-start.2
  11.3 9.0 %broadcast_select_fusion = f32[32,256,5,128]{3,1,2,0:T(8,128)} fusion(pred[32,5]{1,0:T(8,128)(4,1)S(1)} %iota_compare_fusion, bf16[32,5,128,128]{3,2,1,0:T(8,128)(2,1)S(1)} %copy-done.3, bf16[32,128,256]{2,1,0:T(8,128)(2,1)S(1)} %convolution_convert_fusion), kind=kOutput, calls=%fused_computation.4 | convolution fusion | flops 1347420160 | bytes 28311712 | tf_op jit(solution)/shard_map/kpab,kbr->kpar/dot_general | solution.py:24
  20.3 0.0 copy-done.2
  20.3 21.2 %copy.29 = f32[160,128,256]{2,1,0:T(8,128)} copy(f32[160,128,256]{1,2,0:T(8,128)} %bitcast.45) | data formatting | bytes 41943040 | tf_op jit(solution)/shard_map/reshape | solution.py:26
  41.5 0.2 broadcast_in_dim.40
  41.7 0.0 copy-start.6
  41.7 0.0 copy-start.7
  41.7 30.2 %scatter_fusion = f32[16,128,256]{2,1,0:T(8,128)S(1)} fusion(f32[16,128,256]{2,1,0:T(8,128)S(1)} %broadcast_in_dim.40, s32[160]{0:T(256)S(1)} %bitcast.50, f32[160,128,256]{2,1,0:T(8,128)} %copy.29), kind=kCustom, calls=%fused_computation.1 | custom fusion | flops 5242880 | bytes 62915200 | tf_op jit(solution)/shard_map/scatter-add | solution.py:38
  71.9 0.0 copy-start.9
  72.0 0.0 copy-start.8
  72.0 1.1 convert_element_type.59
  73.1 0.0 reduce-scatter.4.cloned.1.call-update
  73.1 0.0 reduce-scatter.6.cloned.1.call-start
  73.1 66.3 %reduce-scatter.4.cloned.1.call-done = bf16[2,128,256]{2,1,0:T(8,128)(2,1)} async-done(((bf16[16,128,256]{2,1,0:T(8,128)(2,1)}), bf16[2,128,256]{2,1,0:T(8,128)(2,1)}) %reduce-scatter.4.cloned.1.call-update) | async-done | bytes 131088 | tf_op jit(solution)/shard_map/reduce_scatter | solution.py:40
  139.4 0.8 slice.35
  140.3 0.0 collective-permute-start
  140.3 0.0 copy-done.6
  140.3 0.2 copy.44
  140.4 1.1 collective-permute-done
  141.5 0.0 copy-done.7
  141.5 0.9 subtract_convert_fusion
  142.4 31.3 %all_gather.6 = bf16[8,128,256]{2,1,0:T(8,128)(2,1)S(1)} all-gather(bf16[1,128,256]{2,1,0:T(8,128)(2,1)S(1)} %subtract_convert_fusion), channel_id=1, replica_groups=mesh['leaf'=4,'front'=8] {'front'}, dimensions={0}, use_global_device_ids=true | all-gather | bytes 589824 | tf_op jit(solution)/shard_map/all_gather | solution.py:46
  173.7 0.3 convolution_convert_fusion.2
  174.0 1.1 fusion.10
  175.1 0.0 reduce-scatter.6.cloned.1.call-update
  175.1 0.0 reduce-scatter.8.cloned.1.call-start
  175.2 0.1 copy.32
  175.3 0.1 reshape.121
  175.4 0.0 copy-done.9
  175.4 0.6 constant_dynamic-slice_fusion
  177.9 58.3 %reduce-scatter.6.cloned.1.call-done = bf16[1,128,256]{1,2,0:T(8,128)(2,1)} async-done(((bf16[8,128,256]{1,2,0:T(8,128)(2,1)}), bf16[1,128,256]{1,2,0:T(8,128)(2,1)}) %reduce-scatter.6.cloned.1.call-update) | async-done | bytes 65552 | tf_op jit(solution)/shard_map/reduce_scatter | solution.py:66
  236.3 0.9 copy.31
  237.2 31.5 %all_gather.7 = bf16[8,128,256]{2,1,0:T(8,128)(2,1)S(1)} all-gather(bf16[1,128,256]{2,1,0:T(8,128)(2,1)S(1)} %copy.31), channel_id=1, replica_groups=mesh['leaf'=4,'front'=8] {'front'}, dimensions={0}, use_global_device_ids=true | all-gather | bytes 589824 | tf_op jit(solution)/shard_map/all_gather | solution.py:75
  268.7 0.0 collective-permute-start.1
  268.7 0.0 copy-done.8
  268.7 0.7 and_reduce_fusion
  269.4 0.7 select_bitcast_fusion
  270.1 0.1 copy.36
  270.3 0.0 copy-start.4
  270.3 0.8 copy-done.4
  271.1 0.0 reduce-scatter.8.cloned.1.call-update
  271.1 1.6 copy.38
  272.7 0.0 collective-permute-done.1
  272.7 0.1 broadcast_select_fusion.2
  272.8 0.1 pad_maximum_fusion
  272.9 7.5 %gather_fusion = bf16[160,128,256]{2,1,0:T(8,128)(2,1)} fusion(bf16[16,128,256]{2,1,0:T(8,128)(2,1)S(1)} %pad_maximum_fusion, s32[1024]{0:T(1024)S(1)} %pad_clamp_fusion), kind=kCustom, calls=%fused_computation | custom fusion | bytes 20972160 | tf_op jit(solution)/shard_map/gather | solution.py:80
  280.4 0.0 copy-start.5
  280.4 14.6 %copy.33 = bf16[32,5,128,256]{2,3,1,0:T(8,128)(2,1)} copy(bf16[32,5,128,256]{3,2,1,0:T(8,128)(2,1)} %bitcast.46) | data formatting | bytes 20971520 | tf_op jit(solution)/shard_map/gather | solution.py:80
  295.0 0.0 copy-done.5
  295.0 0.0 copy-start.1
  295.0 9.2 %convert_bitcast_fusion = bf16[32,128,256]{1,2,0:T(8,128)(2,1)} fusion(bf16[32,128,128]{2,1,0:T(8,128)(2,1)S(1)} %copy-done.5, bf16[32,128,256]{2,1,0:T(8,128)(2,1)} %copy-done.2, bf16[32,5,128,128]{3,2,1,0:T(8,128)(2,1)} %param.12, bf16[32,5,128,256]{2,3,1,0:T(8,128)(2,1)} %copy.33, pred[32,5]{1,0:T(8,128)(4,1)S(1)} %iota_compare_fusion), kind=kOutput, calls=%fused_computation.10 | convolution fusion | flops 1620049920 | bytes 20971680 | tf_op jit(solution)/shard_map/kba,kbr->kar/dot_general | solution.py:84
  304.2 4.1 %copy.37 = bf16[32,128,256]{2,1,0:T(8,128)(2,1)} copy(bf16[32,128,256]{1,2,0:T(8,128)(2,1)} %convert_bitcast_fusion) | data formatting | bytes 4194304
  308.3 24.1 %reduce-scatter.8.cloned.1.call-done = bf16[1,128,256]{2,1,0:T(8,128)(2,1)} async-done(((bf16[8,128,256]{2,1,0:T(8,128)(2,1)}), bf16[1,128,256]{2,1,0:T(8,128)(2,1)}) %reduce-scatter.8.cloned.1.call-update) | async-done | bytes 65552 | tf_op jit(solution)/shard_map/reduce_scatter | solution.py:61
  332.4 0.0 copy-done.1
  (4 shorter events, 0.1 us)
Async XLA Ops:
  7.2 2.0 copy-start
  7.2 132.2 %reduce-scatter.4.cloned.1.call-start = ((), (), s32[]{:S(2)}) async-start(), calls=%async_computation.3 | async-start | bytes 1179648 | tf_op jit(solution)/shard_map/reduce_scatter | solution.py:40
  8.3 3.0 copy-start.3
  11.3 9.0 %copy-start.2 = (bf16[32,128,256]{2,1,0:T(8,128)(2,1)}, bf16[32,128,256]{2,1,0:T(8,128)(2,1)S(1)}, u32[]{:S(2)}) copy-start(bf16[32,128,256]{2,1,0:T(8,128)(2,1)S(1)} %convolution_convert_fusion) | copy-start | bytes 6291460
  41.7 98.6 %copy-start.6 = (bf16[1,128,1024]{2,1,0:T(8,128)(2,1)S(1)}, bf16[1,128,1024]{2,1,0:T(8,128)(2,1)}, u32[]{:S(2)}) copy-start(bf16[1,128,1024]{2,1,0:T(8,128)(2,1)} %param.17) | copy-start | bytes 786436
  41.7 99.8 %copy-start.7 = (bf16[1,128,256]{2,1,0:T(8,128)(2,1)S(1)}, bf16[1,128,256]{2,1,0:T(8,128)(2,1)}, u32[]{:S(2)}) copy-start(bf16[1,128,256]{2,1,0:T(8,128)(2,1)} %param.15) | copy-start | bytes 196612
  71.9 103.4 %copy-start.9 = (s32[1,8]{1,0:T(1,128)S(1)}, s32[1,8]{1,0:T(1,128)}, u32[]{:S(2)}) copy-start(s32[1,8]{1,0:T(1,128)} %param.16) | copy-start | bytes 100
  72.0 196.7 %copy-start.8 = (s32[3]{0:T(128)S(1)}, s32[3]{0:T(128)}, u32[]{:S(2)}) copy-start(s32[3]{0:T(128)} %constant.101.clone.1) | copy-start | bytes 40
  73.1 163.2 %reduce-scatter.6.cloned.1.call-start = ((), (), s32[]{:S(2)}) async-start(), calls=%async_computation.4 | async-start | bytes 589824 | tf_op jit(solution)/shard_map/reduce_scatter | solution.py:66
  140.3 1.3 collective-permute-start
  175.1 157.3 %reduce-scatter.8.cloned.1.call-start = ((), (), s32[]{:S(2)}) async-start(), calls=%async_computation.5 | async-start | bytes 589824 | tf_op jit(solution)/shard_map/reduce_scatter | solution.py:61
  268.7 4.0 %collective-permute-start.1 = (bf16[8,128,256]{2,1,0:T(8,128)(2,1)S(1)}, bf16[8,128,256]{2,1,0:T(8,128)(2,1)S(1)}, u32[]{:S(2)}, u32[]{:S(2)}) collective-permute-start(bf16[8,128,256]{2,1,0:T(8,128)(2,1)S(1)} %all_gather.7), channel_id=1, source_target_pairs={{0,8},{8,0},{16,24},{24,16},{1,9},{9,1},{17,25},{25,17},{2,10},{10... | collective-permute-start | bytes 1572872 | tf_op jit(solution)/shard_map/ppermute | solution.py:8
  270.3 0.8 copy-start.4
  280.4 14.6 %copy-start.5 = (bf16[32,128,128]{2,1,0:T(8,128)(2,1)S(1)}, bf16[32,128,128]{2,1,0:T(8,128)(2,1)}, u32[]{:S(2)}) copy-start(bf16[32,128,128]{2,1,0:T(8,128)(2,1)} %param.10) | copy-start | bytes 3145732
  295.0 37.4 %copy-start.1 = (bf16[32,128,256]{2,1,0:T(8,128)(2,1)S(1)}, bf16[32,128,256]{2,1,0:T(8,128)(2,1)}, u32[]{:S(2)}) copy-start(bf16[32,128,256]{2,1,0:T(8,128)(2,1)} %param.11) | copy-start | bytes 6291460
Sparse Core Ops, SparseCore 0:
  73.2 66.1 reduce-scatter.3
  175.3 60.9 reduce-scatter.5
  271.2 61.1 reduce-scatter.7
where the time goes:
time: 341 us; the launch traced here: 339 us
  waiting for transfers between devices  150 us (44%)
  blocking collectives  62.8 us (18%)
  local copies, waits for them, and re-layouts  53.1 us (16%)
  other arithmetic  35.5 us (10%)
  matrix products  21.7 us (6%)
  between operations  15.9 us (5%)
    reduce_scatter x1, waiting for transfers between devices, on_device(): lax.psum_scatter(partial_terms.astype(jnp.bfloat16), 'front', scatter_dim...  66.3 us
    reduce_scatter x1, waiting for transfers between devices, on_device(): lax.psum_scatter(result.reshape(owned_count * lax.axis_size('front'), blo...  58.3 us
    all_gather x1, blocking collectives, on_device(): whole_front = lax.all_gather(solved, 'front', axis=0, tiled=True)  31.5 us
    all_gather x1, blocking collectives, on_device(): arrived = lax.all_gather(separator_in, 'front', axis=0, tiled=True)  31.3 us
    scatter-add x1, other arithmetic, on_device(): partial_terms = jnp.zeros((2 * front_seps, block_width, probe_count), jnp...  30.2 us
    reduce_scatter x1, waiting for transfers between devices, on_device(): lax.psum_scatter(placed.astype(jnp.bfloat16), 'front', scatter_dimension=...  24.1 us
    gather x2, local copies, waits for them, and re-layouts, on_device(): picked = pair_field[block_rows]  22.1 us
    reshape x1, local copies, waits for them, and re-layouts, on_device(): product = product.reshape(-1, block_width, probe_count)  21.2 us
  transfers between devices with their start and end apart: 5, of which 4 were waited for; matrix products, arithmetic and copies ran while one was open for 12% of the time, Pallas kernels for 0%

commit v1 on v0

v1 whole, which is shorter than its diff:
```python
import functools
import math

import jax
import jax.numpy as jnp
from jax import lax
from jax.experimental import pallas as pl
from jax.experimental.pallas import tpu as pltpu
from jax.sharding import PartitionSpec as P

MESH = pl.DeviceIdType.MESH
F32 = jnp.float32
BF16 = jnp.bfloat16
LEAF_STEP = 4
VMEM_BYTES = 56 * 1024 * 1024
FIRST_DIMS = (((0,), (0,)), ((), ()))


def leaf_forward(rows_ref, fill_ref, inverse_ref, rhs_ref, off_ref, forward_ref, partial_ref, acc):
    step = pl.program_id(0)
    seps = partial_ref.shape[0]
    slots, width = off_ref.shape[1], off_ref.shape[2]

    @pl.when(step == 0)
    def _():
        acc[...] = jnp.zeros_like(acc)

    for i in range(LEAF_STEP):
        leaf = step * LEAF_STEP + i
        forward = jnp.dot(inverse_ref[i], rhs_ref[i], preferred_element_type=F32).astype(BF16)
        forward_ref[i] = forward
        product = jnp.dot(
            off_ref[i].reshape(slots * width, width), forward, preferred_element_type=F32
        )
        for p in range(slots):
            target = jnp.where(p < fill_ref[leaf], rows_ref[leaf, p], seps)
            acc[target] += product[p * width : (p + 1) * width]

    @pl.when(step == pl.num_programs(0) - 1)
    def _():
        partial_ref[...] = acc[:seps].astype(BF16)


def leaf_backward(rows_ref, fill_ref, field_ref, inverse_ref, off_ref, forward_ref, out_ref):
    step = pl.program_id(0)
    slots, width = off_ref.shape[1], off_ref.shape[2]
    for i in range(LEAF_STEP):
        leaf = step * LEAF_STEP + i
        picked = []
        for p in range(slots):
            block = field_ref[rows_ref[leaf, p]]
            picked.append(jnp.where(p < fill_ref[leaf], block, jnp.zeros_like(block)))
        pulled = lax.dot_general(
            off_ref[i].reshape(slots * width, width),
            jnp.concatenate(picked, axis=0),
            FIRST_DIMS,
            preferred_element_type=F32,
        )
        backward = (forward_ref[i].astype(F32) - pulled).astype(BF16)
        out_ref[i] = lax.dot_general(
            inverse_ref[i], backward, FIRST_DIMS, preferred_element_type=F32
        ).astype(BF16)


def separators(
    zs, xs, order_ref, partial_ref, rhs_ref, panel_ref, column_ref,
    field_ref, forward_ref, solution_ref,
    from_core, to_x, from_x, to_z, from_z, gathered_in, gathered_fwd,
    core_send, core_recv, x_send, x_recv, z_send, z_recv,
    in_sems, fwd_sems, sol_sems, sib_send, sib_recv,
):
    fronts = zs * xs
    width = rhs_ref.shape[1]
    leaf, me = lax.axis_index("leaf"), lax.axis_index("front")
    half = lax.rem(leaf, 2)
    z, x = me // xs, lax.rem(me, xs)
    sibling = (leaf + 1 - 2 * half, me)

    def at(zz, xx):
        return (leaf, zz * xs + xx)

    other_z = [lax.rem(z + k, zs) for k in range(1, zs)]
    other_x = [lax.rem(x + k, xs) for k in range(1, xs)]

    barrier = pltpu.get_barrier_semaphore()
    peers = [at(zz, x) for zz in other_z] + [at(z, xx) for xx in other_x] + [sibling]
    for peer in peers:
        pl.semaphore_signal(barrier, inc=1, device_id=peer, device_id_type=MESH)
    pl.semaphore_wait(barrier, len(peers))

    sent = []

    def remote(src, dst, send, recv, device):
        return pltpu.make_async_remote_copy(
            src_ref=src, dst_ref=dst, send_sem=send, recv_sem=recv,
            device_id=device, device_id_type=MESH,
        )

    def push(src, dst, send, recv, device):
        copy = remote(src, dst, send, recv, device)
        copy.start()
        sent.append(copy)

    def arrived(dst, recv):
        remote(dst, dst, recv, recv, sibling).wait_recv()

    order = other_z + [z]
    for zz in order:
        push(
            partial_ref.at[pl.ds((1 - half) * fronts + zz * xs, xs)],
            from_core.at[pl.ds(zz * xs, xs)],
            core_send.at[zz], core_recv.at[zz], sibling,
        )
    for zz in order:
        arrived(from_core.at[pl.ds(zz * xs, xs)], core_recv.at[zz])
        for xx in other_x:
            f = zz * xs + xx
            to_x[f] = (
                partial_ref[half * fronts + f].astype(F32) + from_core[f].astype(F32)
            ).astype(BF16)
            push(
                to_x.at[f], from_x.at[zz * xs + x], x_send.at[f], x_recv.at[zz * xs + x], at(z, xx)
            )
    total = None
    for zz in order:
        f = zz * xs + x
        total = partial_ref[half * fronts + f].astype(F32) + from_core[f].astype(F32)
        for xx in other_x:
            arrived(from_x.at[zz * xs + xx], x_recv.at[zz * xs + xx])
            total += from_x[zz * xs + xx].astype(F32)
        if zz is not z:
            to_z[zz] = total.astype(BF16)
            push(to_z.at[zz], from_z.at[z], z_send.at[zz], z_recv.at[z], at(zz, x))
    for zz in other_z:
        arrived(from_z.at[zz], z_recv.at[zz])
        total += from_z[zz].astype(F32)

    def gather(buffer, base, sems, use):
        z_out, z_in, x_out, x_in = sems
        own = buffer.at[base + me]
        for xx in other_x:
            push(own, own, x_out.at[z * xs + xx], x_in.at[me], at(z, xx))
        for zz in other_z:
            push(own, own, z_out.at[zz], z_in.at[z], at(zz, x))
        use(me)
        for zz in other_z:
            f = zz * xs + x
            block = buffer.at[base + f]
            arrived(block, z_in.at[zz])
            for xx in other_x:
                push(block, block, x_out.at[zz * xs + xx], x_in.at[f], at(z, xx))
            use(f)
        for zz in [z] + other_z:
            for xx in other_x:
                f = zz * xs + xx
                arrived(buffer.at[base + f], x_in.at[f])
                use(f)

    result = []

    def add(matrix_of, vectors):
        def use(f):
            term = jnp.dot(matrix_of(f), vectors[f], preferred_element_type=F32)
            result[:] = [result[0] + term] if result else [term]

        return use

    gathered_in[me] = (rhs_ref[0].astype(F32) - total).astype(BF16)
    gather(gathered_in, 0, in_sems, add(lambda f: panel_ref[f], gathered_in))
    gathered_fwd[me] = result.pop().astype(BF16)
    gather(gathered_fwd, 0, fwd_sems, add(lambda f: column_ref[f], gathered_fwd))
    solved = result.pop()
    base = half * fronts
    field_ref[base + me] = solved.astype(BF16)

    def to_sibling(f):
        block = field_ref.at[base + f]
        push(block, block, sib_send.at[f], sib_recv.at[f], sibling)

    gather(field_ref, base, sol_sems, to_sibling)
    solution_ref[0] = solved
    slot = jnp.int32(0)
    for p in range(fronts):
        slot = jnp.where(order_ref[0, p] == me, p, slot)
    forward_ref[0] = gathered_fwd[slot]
    for zz in [z] + other_z:
        for xx in [x] + other_x:
            f = zz * xs + xx
            arrived(field_ref.at[(1 - half) * fronts + f], sib_recv.at[f])
    for copy in sent:
        copy.wait_send()


def on_device(
    leaf_inverse, leaf_rhs, off_blocks, block_rows, fill_count, sep_rhs, panel_order, sep_inverse
):
    leaves, width = leaf_inverse.shape[:2]
    probes = leaf_rhs.shape[2]
    slots = off_blocks.shape[1]
    fronts = lax.axis_size("front")
    xs = math.isqrt(fronts // 2)
    zs = fronts // xs
    steps = leaves // LEAF_STEP
    block = (width, probes)
    panel = sep_inverse.reshape(width, fronts, width)
    columns = lax.all_to_all(jnp.transpose(panel, (1, 2, 0)), "front", 0, 0, tiled=True)
    panel = jnp.transpose(panel, (1, 0, 2))

    smem = pl.BlockSpec(memory_space=pltpu.SMEM)
    vmem = pl.BlockSpec(memory_space=pltpu.VMEM)
    inverse_spec = pl.BlockSpec((LEAF_STEP, width, width), lambda i: (i, 0, 0))
    vector_spec = pl.BlockSpec((LEAF_STEP,) + block, lambda i: (i, 0, 0))
    off_spec = pl.BlockSpec((LEAF_STEP, slots, width, width), lambda i: (i, 0, 0, 0))
    flops = 2 * leaves * (slots + 1) * width * width * probes
    moved = 2 * leaves * width * (width * (slots + 1) + 2 * probes)
    cost = pl.CostEstimate(flops=flops, bytes_accessed=moved, transcendentals=0)

    forward, partial = pl.pallas_call(
        leaf_forward,
        grid=(steps,),
        out_shape=(
            jax.ShapeDtypeStruct((leaves,) + block, BF16),
            jax.ShapeDtypeStruct((2 * fronts,) + block, BF16),
        ),
        in_specs=[smem, smem, inverse_spec, vector_spec, off_spec],
        out_specs=(vector_spec, pl.BlockSpec((2 * fronts,) + block, lambda i: (0, 0, 0))),
        scratch_shapes=[pltpu.VMEM((2 * fronts + 1,) + block, F32)],
        compiler_params=pltpu.CompilerParams(vmem_limit_bytes=VMEM_BYTES),
        cost_estimate=cost,
        name="leaf_forward",
    )(block_rows, fill_count, leaf_inverse, leaf_rhs, off_blocks)

    dma = pltpu.SemaphoreType.DMA
    gather_sems = [dma((zs,)), dma((zs,)), dma((fronts,)), dma((fronts,))]

    def kernel(*refs):
        head, sems = refs[:15], list(refs[15:])
        groups = [tuple(sems[6 + 4 * k : 10 + 4 * k]) for k in range(3)]
        separators(zs, xs, *head, *sems[:6], *groups, *sems[18:])

    field, sep_forward, sep_solution = pl.pallas_call(
        kernel,
        out_shape=(
            jax.ShapeDtypeStruct((2 * fronts,) + block, BF16),
            jax.ShapeDtypeStruct((1,) + block, BF16),
            jax.ShapeDtypeStruct((1,) + block, F32),
        ),
        in_specs=[smem, vmem, vmem, vmem, vmem],
        out_specs=(vmem, vmem, vmem),
        scratch_shapes=[
            pltpu.VMEM((fronts,) + block, BF16),
            pltpu.VMEM((fronts,) + block, BF16),
            pltpu.VMEM((fronts,) + block, BF16),
            pltpu.VMEM((zs,) + block, BF16),
            pltpu.VMEM((zs,) + block, BF16),
            pltpu.VMEM((fronts,) + block, BF16),
            pltpu.VMEM((fronts,) + block, BF16),
            dma((zs,)), dma((zs,)), dma((fronts,)), dma((fronts,)), dma((zs,)), dma((zs,)),
            *gather_sems, *gather_sems, *gather_sems,
            dma((fronts,)), dma((fronts,)),
        ],
        compiler_params=pltpu.CompilerParams(
            collective_id=0, has_side_effects=True, vmem_limit_bytes=VMEM_BYTES
        ),
        cost_estimate=pl.CostEstimate(
            flops=4 * fronts * width * width * probes,
            bytes_accessed=8 * fronts * width * probes,
            transcendentals=0,
        ),
        name="separators",
    )(panel_order, partial, sep_rhs, panel, columns)

    leaf_solution = pl.pallas_call(
        leaf_backward,
        grid=(steps,),
        out_shape=jax.ShapeDtypeStruct((leaves,) + block, BF16),
        in_specs=[
            smem, smem, pl.BlockSpec((2 * fronts,) + block, lambda i: (0, 0, 0)),
            inverse_spec, off_spec, vector_spec,
        ],
        out_specs=vector_spec,
        compiler_params=pltpu.CompilerParams(vmem_limit_bytes=VMEM_BYTES),
        cost_estimate=cost,
        name="leaf_backward",
    )(block_rows, fill_count, field, leaf_inverse, off_blocks, forward)
    return (leaf_solution, sep_forward, sep_solution)


def solution(mesh):
    placed = (
        P(("leaf", "front"), None, None),
        P(("leaf", "front"), None, None),
        P(("leaf", "front"), None, None, None),
        P(("leaf", "front"), None),
        P(("leaf", "front")),
        P(("leaf", "front"), None, None),
        P("leaf", None),
        P(("leaf", "front"), None, None),
    )
    return jax.shard_map(
        on_device,
        mesh=mesh,
        in_specs=placed,
        out_specs=(
            P(("leaf", "front"), None, None),
            P(("leaf", "front"), None, None),
            P(("leaf", "front"), None, None),
        ),
        check_vma=False,
    )
```

time: 341 us -> 93.4 us (0.27)
  waiting for transfers between devices: 150 us -> 0.01 us
  Pallas kernels: 0 us -> 77.8 us
  blocking collectives: 62.8 us -> 0 us
  local copies, waits for them, and re-layouts: 53.1 us -> 6.92 us
  other arithmetic: 35.5 us -> 0 us
  matrix products: 21.7 us -> 0 us
  between operations: 15.9 us -> 0.67 us
  starting transfers between devices: 0.13 us -> 7.25 us
    reduce_scatter x3 -> x0, waiting for transfers between devices: 149 us -> none  [the longest x1 66.3 us: on_device(): lax.psum_scatter(partial_terms.astype(jnp.bfloat16), 'front', scatter_dim...]
    pallas_call x0 -> x3, Pallas kernels: none -> 77.8 us  [the longest x1 54.7 us: on_device(): pl.pallas_call(kernel, out_shape=(jax.ShapeDtypeStruct((2 * fronts,) + bl...]
    all_gather x2 -> x0, blocking collectives: 62.8 us -> none  [the longest x1 31.5 us: on_device(): whole_front = lax.all_gather(solved, 'front', axis=0, tiled=True)]
    scatter-add x1 -> x0, other arithmetic: 30.2 us -> none  [on_device(): partial_terms = jnp.zeros((2 * front_seps, block_width, probe_count), jnp...]
    gather x2 -> x0, local copies, waits for them, and re-layouts: 22.1 us -> none  [on_device(): picked = pair_field[block_rows]]
    dot_general x5 -> x0, matrix products: 21.7 us -> none  [the longest x1 9.24 us: on_device(): jnp.einsum('kba,kbr->kar', leaf_inverse, backward, preferred_element_type...]
    reshape x2 -> x0, local copies, waits for them, and re-layouts: 21.3 us -> none  [the longest x1 21.2 us: on_device(): product = product.reshape(-1, block_width, probe_count)]
    all_to_all x0 -> x1, starting transfers between devices: none -> 7.25 us  [on_device(): lax.all_to_all(jnp.transpose(panel, (1, 2, 0)), 'front', 0, 0, tiled=True)]
  transfers between devices with their start and end apart: 5 -> 1, of which waited for: 4 -> 0; matrix products, arithmetic and copies ran while one was open for 12% -> 3% of each run, Pallas kernels for 0% -> 12%
where the time goes in v1:
time: 93.4 us; the launch traced here: 92.6 us
  Pallas kernels  77.8 us (83%)
  starting transfers between devices  7.25 us (8%)
  local copies, waits for them, and re-layouts  6.92 us (7%)
    pallas_call x1, Pallas kernels, on_device(): pl.pallas_call(kernel, out_shape=(jax.ShapeDtypeStruct((2 * fronts,) + bl...  54.7 us
    pallas_call x1, Pallas kernels, on_device(): pl.pallas_call(leaf_backward, grid=(steps,), out_shape=jax.ShapeDtypeStru...  11.9 us
    pallas_call x1, Pallas kernels, on_device(): pl.pallas_call(leaf_forward, grid=(steps,), out_shape=(jax.ShapeDtypeStru...  11.2 us
    all_to_all x1, starting transfers between devices, on_device(): lax.all_to_all(jnp.transpose(panel, (1, 2, 0)), 'front', 0, 0, tiled=True)  7.25 us
    unnamed x10, local copies, waits for them, and re-layouts  5.13 us
  transfers between devices with their start and end apart: 1, of which 0 were waited for; matrix products, arithmetic and copies ran while one was open for 3% of the time, Pallas kernels for 12%

profile of v1, /device:TPU:0, one launch (start us, length us, event | category | flops | bytes accessed | tf_op | source)
XLA Modules:
  0.0 92.6 jit_solution(268352615896361476)
XLA Ops:
  0.6 1.8 %copy.12 = bf16[1,128,1024]{1,2,0:T(8,128)(2,1)} copy(bf16[1,128,1024]{2,1,0:T(8,128)(2,1)} %param.15) | data formatting | bytes 524288 | tf_op args[7]
  2.4 7.3 %all-to-all-start = ((bf16[8,128,128]{2,1,0:T(8,128)(2,1)}), bf16[8,128,128]{2,1,0:T(8,128)(2,1)S(1)}, u32[]{:S(2)}, u32[]{:S(2)}) async-start(bf16[8,128,128]{2,1,0:T(8,128)(2,1)} %bitcast.2), calls=%async_computation | async-start | bytes 524288 | tf_op jit(solution)/shard_map/all_to_all | solution.py:206
  9.7 1.4 %copy.14.rows_ref = s32[32,5]{1,0:T(8,128)} copy(s32[32,5]{0,1:T(8,128)} %param.11) | data formatting | bytes 1280 | tf_op args[3]
  11.0 1.8 %copy.13.refs_3_ = bf16[8,128,128]{2,1,0:T(8,128)(2,1)} copy(bf16[8,128,128]{1,2,0:T(8,128)(2,1)} %bitcast.1) | data formatting | bytes 524288 | tf_op jit(solution)/shard_map/transpose | solution.py:207
  12.8 11.2 %leaf_forward.1 = (bf16[32,128,256]{2,1,0:T(8,128)(2,1)}, bf16[16,128,256]{2,1,0:T(8,128)(2,1)}) custom-call(s32[32,5]{1,0:T(8,128)} %copy.14.rows_ref, s32[32]{0:T(128)} %fill_ref.3, bf16[32,128,128]{2,1,0:T(8,128)(2,1)} %inverse_ref.3, bf16[32,128,256]{2,1,0:T(8,128)(2,1)} %rhs_ref.1, bf16[32,5,128,128]{3,2,1,0:T(8,128)(2,1)} %off_ref.3), custom_call_target="tpu_custom_call" | custom-call | flops 1610612736 | bytes 10485760 | tf_op jit(solution)/shard_map/leaf_forward/pallas_call | solution.py:218
  24.0 0.0 all-to-all-done.refs_4_
  24.0 0.0 copy-start
  24.0 0.7 copy-done
  24.7 54.7 %separators.1 = (bf16[16,128,256]{2,1,0:T(8,128)(2,1)}, bf16[1,128,256]{2,1,0:T(8,128)(2,1)}, f32[1,128,256]{2,1,0:T(8,128)}) custom-call(s32[1,8]{1,0:T(1,128)} %refs_0_.1, bf16[16,128,256]{2,1,0:T(8,128)(2,1)} %get-tuple-element.8.refs_1_, bf16[1,128,256]{2,1,0:T(8,128)(2,1)} %refs_2_.1, bf16[8,128,128]{2,1,0:T(8,128)(2,1)} %copy.13.refs_3_, ...), custom_call_target="tpu_custom_call" | custom-call | flops 134217728 | bytes 2097152 | tf_op jit(solution)/shard_map/separators/pallas_call | solution.py:241
  79.4 0.0 copy-start.2
  79.4 0.0 copy-start.1
  79.4 11.9 %leaf_backward.1 = bf16[32,128,256]{2,1,0:T(8,128)(2,1)} custom-call(s32[32,5]{1,0:T(8,128)} %copy.14.rows_ref, s32[32]{0:T(128)} %fill_ref.3, bf16[16,128,256]{2,1,0:T(8,128)(2,1)} %get-tuple-element.9.field_ref, bf16[32,128,128]{2,1,0:T(8,128)(2,1)} %inverse_ref.3, bf16[32,5,128,128]{3,2,1,0:T(8,128)(2,1)} %off_ref.3, ...), custom_call_target="tpu_custom_call" | custom-call | flops 1610612736 | bytes 10485760 | tf_op jit(solution)/shard_map/leaf_backward/pallas_call | solution.py:273
  91.3 0.0 copy-done.2
  91.3 0.6 copy.17
  92.0 0.0 copy-done.1
  92.0 0.7 copy.18
Async XLA Ops:
  2.4 21.6 %all-to-all-start = ((bf16[8,128,128]{2,1,0:T(8,128)(2,1)}), bf16[8,128,128]{2,1,0:T(8,128)(2,1)S(1)}, u32[]{:S(2)}, u32[]{:S(2)}) async-start(bf16[8,128,128]{2,1,0:T(8,128)(2,1)} %bitcast.2), calls=%async_computation | async-start | bytes 524288 | tf_op jit(solution)/shard_map/all_to_all | solution.py:206
  24.0 0.7 copy-start
  79.4 12.0 %copy-start.2 = (bf16[1,128,256]{2,1,0:T(8,128)(2,1)S(1)}, bf16[1,128,256]{2,1,0:T(8,128)(2,1)}, u32[]{:S(2)}) copy-start(bf16[1,128,256]{2,1,0:T(8,128)(2,1)} %get-tuple-element.17) | copy-start | bytes 196612
  79.4 12.6 %copy-start.1 = (f32[1,128,256]{2,1,0:T(8,128)S(1)}, f32[1,128,256]{2,1,0:T(8,128)}, u32[]{:S(2)}) copy-start(f32[1,128,256]{2,1,0:T(8,128)} %get-tuple-element.18) | copy-start | bytes 393220

commit v2 on v1

v2 whole, which is shorter than its diff:
```python
import jax
import jax.numpy as jnp
from jax import lax
from jax.experimental import pallas as pl
from jax.experimental.pallas import tpu as pltpu
from jax.sharding import PartitionSpec as P

MESH = pl.DeviceIdType.MESH
F32 = jnp.float32
BF16 = jnp.bfloat16
LEAF_STEP = 4
VMEM_BYTES = 56 * 1024 * 1024
FIRST_DIMS = (((0,), (0,)), ((), ()))


def leaf_forward(rows_ref, fill_ref, inverse_ref, rhs_ref, off_ref, forward_ref, partial_ref, acc):
    step = pl.program_id(0)
    chunks, seps, _, lanes = partial_ref.shape
    slots, width = off_ref.shape[1], off_ref.shape[2]

    @pl.when(step == 0)
    def _():
        acc[...] = jnp.zeros_like(acc)

    for i in range(LEAF_STEP):
        leaf = step * LEAF_STEP + i
        forward = jnp.dot(inverse_ref[i], rhs_ref[i], preferred_element_type=F32).astype(BF16)
        forward_ref[i] = forward
        product = jnp.dot(
            off_ref[i].reshape(slots * width, width), forward, preferred_element_type=F32
        )
        for p in range(slots):
            target = jnp.where(p < fill_ref[leaf], rows_ref[p, leaf], seps)
            acc[target] += product[p * width : (p + 1) * width]

    @pl.when(step == pl.num_programs(0) - 1)
    def _():
        for c in range(chunks):
            partial_ref[c] = acc[:seps, :, c * lanes : (c + 1) * lanes].astype(BF16)


def leaf_backward(
    rows_ref, fill_ref, field_ref, inverse_ref, off_ref, forward_ref, sep_fwd_ref, sep_sol_ref,
    out_ref, sep_fwd_out, sep_sol_out,
):
    step = pl.program_id(0)
    slots, width = off_ref.shape[1], off_ref.shape[2]

    @pl.when(step == 0)
    def _():
        sep_fwd_out[...] = sep_fwd_ref[...]
        sep_sol_out[...] = sep_sol_ref[...]

    for i in range(LEAF_STEP):
        leaf = step * LEAF_STEP + i
        picked = []
        for p in range(slots):
            row = rows_ref[p, leaf]
            block = jnp.concatenate([field_ref[c, row] for c in range(field_ref.shape[0])], axis=1)
            picked.append(jnp.where(p < fill_ref[leaf], block, jnp.zeros_like(block)))
        pulled = lax.dot_general(
            off_ref[i].reshape(slots * width, width),
            jnp.concatenate(picked, axis=0),
            FIRST_DIMS,
            preferred_element_type=F32,
        )
        backward = (forward_ref[i].astype(F32) - pulled).astype(BF16)
        out_ref[i] = lax.dot_general(
            inverse_ref[i], backward, FIRST_DIMS, preferred_element_type=F32
        ).astype(BF16)


def separators(
    order_ref, partial_ref, rhs_ref, panel_ref, peer_panel_ref,
    field_ref, forward_ref, solution_ref,
    from_core, to_x, from_x, to_z, from_z, gathered_in, to_adjoint, from_adjoint, gathered_fwd,
    to_peer, from_peer, panel_t,
    core_send, core_recv, x_send, x_recv, z_send, z_recv, in_send, in_recv, adj_send, adj_recv,
    fwd_send, fwd_recv, sol_send, sol_recv, sol_x_send, sol_x_recv, sib_send, sib_recv,
    peer_send, peer_recv,
):
    chunks, seps, width, lanes = partial_ref.shape
    fronts = seps // 2
    lines = fronts // chunks
    leaf, me = lax.axis_index("leaf"), lax.axis_index("front")
    half = lax.rem(leaf, 2)
    line, part = me // chunks, lax.rem(me, chunks)
    base, far_base = half * fronts, (1 - half) * fronts
    sibling = (leaf + 1 - 2 * half, me)
    others = [lax.rem(line + k, lines) for k in range(1, lines)]
    parts = [lax.rem(part + k, chunks) for k in range(1, chunks)]
    order = others + [line]

    def along(ll):
        return (leaf, ll * chunks + part)

    def across(pp):
        return (leaf, line * chunks + pp)

    def group(ll, start=0):
        return pl.ds(start + ll * chunks, chunks)

    barrier = pltpu.get_barrier_semaphore()
    peers = [along(ll) for ll in others] + [across(pp) for pp in parts] + [sibling]
    for peer in peers:
        pl.semaphore_signal(barrier, inc=1, device_id=peer, device_id_type=MESH)
    pl.semaphore_wait(barrier, len(peers))

    sent = []

    def remote(src, dst, send, recv, device):
        return pltpu.make_async_remote_copy(
            src_ref=src, dst_ref=dst, send_sem=send, recv_sem=recv,
            device_id=device, device_id_type=MESH,
        )

    def push(src, dst, send, recv, device):
        copy = remote(src, dst, send, recv, device)
        copy.start()
        sent.append(copy)

    def arrived(dst, recv):
        remote(dst, dst, recv, recv, sibling).wait_recv()

    rhs = [rhs_ref[0, :, c * lanes : (c + 1) * lanes].astype(F32) for c in range(chunks)]

    def rhs_of(pp):
        value = rhs[0]
        for c in range(1, chunks):
            value = jnp.where(pp == c, rhs[c], value)
        return value

    for pp in parts + [part]:
        for ll in order:
            push(
                partial_ref.at[pp, group(ll, far_base)], from_core.at[pp, group(ll)],
                core_send.at[pp, ll], core_recv.at[pp, ll], sibling,
            )

    def pair_sum(pp, f):
        return partial_ref[pp, base + f].astype(F32) + from_core[pp, f].astype(F32)

    for pp in parts:
        for ll in order:
            arrived(from_core.at[pp, group(ll)], core_recv.at[pp, ll])
            for k in range(chunks):
                f = ll * chunks + k
                value = pair_sum(pp, f)
                if ll is line:
                    value = jnp.where(part == k, value - rhs_of(pp), value)
                to_x[pp, f] = value.astype(BF16)
            push(
                to_x.at[pp, group(ll)], from_x.at[part, group(ll)],
                x_send.at[pp, ll], x_recv.at[part, ll], across(pp),
            )
    totals = []
    for ll in order:
        arrived(from_core.at[part, group(ll)], core_recv.at[part, ll])
        for pp in parts:
            arrived(from_x.at[pp, group(ll)], x_recv.at[pp, ll])
        for k in range(chunks):
            f = ll * chunks + k
            value = pair_sum(part, f)
            for pp in parts:
                value += from_x[pp, f].astype(F32)
            if ll is line:
                totals.append(jnp.where(part == k, value - rhs_of(part), value))
            else:
                to_z[f] = value.astype(BF16)
        if ll is not line:
            push(to_z.at[group(ll)], from_z.at[group(line)], z_send.at[ll], z_recv.at[line], along(ll))
    for ll in others:
        arrived(from_z.at[group(ll)], z_recv.at[ll])
        for k in range(chunks):
            totals[k] += from_z[ll * chunks + k].astype(F32)

    for k in range(chunks):
        gathered_in[line * chunks + k] = (-totals[k]).astype(BF16)
    mine = group(line)
    for ll in others:
        push(gathered_in.at[mine], gathered_in.at[mine], in_send.at[ll], in_recv.at[line], along(ll))

    panels = [panel_ref] + [peer_panel_ref.at[k] for k in range(chunks - 1)]
    for f in range(fronts):
        for k, panel in enumerate(panels):
            panel_t[f * width : (f + 1) * width, k * width : (k + 1) * width] = panel[
                :, f * width : (f + 1) * width
            ].T

    forward = [jnp.zeros((width, lanes), F32)] * chunks
    for ll in [line] + others:
        if ll is not line:
            arrived(gathered_in.at[group(ll)], in_recv.at[ll])
        vectors = gathered_in[group(ll)].reshape(chunks * width, lanes)
        columns = pl.ds(pl.multiple_of(ll * chunks * width, chunks * width), chunks * width)
        for k, panel in enumerate(panels):
            forward[k] += jnp.dot(panel[:, columns], vectors, preferred_element_type=F32)
    forward = [value.astype(BF16) for value in forward]
    stacked = jnp.concatenate(forward, axis=0)
    for k in range(chunks):
        gathered_fwd[line * chunks + lax.rem(part + k, chunks)] = forward[k]

    solved = None
    for ll in order:
        rows = pl.ds(pl.multiple_of(ll * chunks * width, chunks * width), chunks * width)
        term = jnp.dot(panel_t[rows, :], stacked, preferred_element_type=F32)
        if ll is line:
            solved = term
        else:
            to_adjoint[group(ll)] = term.astype(BF16).reshape(chunks, width, lanes)
            push(
                to_adjoint.at[group(ll)], from_adjoint.at[mine],
                adj_send.at[ll], adj_recv.at[line], along(ll),
            )
    for ll in others:
        arrived(from_adjoint.at[group(ll)], adj_recv.at[ll])
        solved += from_adjoint[group(ll)].reshape(chunks * width, lanes).astype(F32)

    def share(pp, ll):
        block = field_ref.at[pp, group(ll, base)]
        push(block, block, sib_send.at[pp, ll], sib_recv.at[pp, ll], sibling)

    def share_across(ll):
        block = field_ref.at[part, group(ll, base)]
        for pp in parts:
            push(block, block, sol_x_send.at[pp, ll], sol_x_recv.at[part, ll], across(pp))

    field_ref[part, group(line, base)] = solved.astype(BF16).reshape(chunks, width, lanes)
    own = field_ref.at[part, group(line, base)]
    for ll in others:
        push(own, own, sol_send.at[ll], sol_recv.at[line], along(ll))
    share_across(line)
    share(part, line)
    for ll in others:
        push(
            gathered_fwd.at[mine], gathered_fwd.at[mine],
            fwd_send.at[ll], fwd_recv.at[line], along(ll),
        )
    for ll in others:
        arrived(field_ref.at[part, group(ll, base)], sol_recv.at[ll])
        share_across(ll)
        share(part, ll)
    for ll in [line] + others:
        for pp in parts:
            arrived(field_ref.at[pp, group(ll, base)], sol_x_recv.at[pp, ll])
            share(pp, ll)
    for c in range(chunks):
        solution_ref[0, :, c * lanes : (c + 1) * lanes] = field_ref[c, base + me].astype(F32)

    for ll in others:
        arrived(gathered_fwd.at[group(ll)], fwd_recv.at[ll])

    def forward_of(sep):
        slot = jnp.int32(0)
        for p in range(fronts):
            slot = jnp.where(order_ref[0, p] == sep, p, slot)
        return gathered_fwd[slot]

    from_peer[part] = forward_of(me)
    for pp in parts:
        to_peer[pp] = forward_of(line * chunks + pp)
        push(to_peer.at[pp], from_peer.at[part], peer_send.at[pp], peer_recv.at[part], across(pp))
    for pp in parts + [part]:
        for ll in [line] + others:
            arrived(field_ref.at[pp, group(ll, far_base)], sib_recv.at[pp, ll])
    for pp in parts:
        arrived(from_peer.at[pp], peer_recv.at[pp])
    for c in range(chunks):
        forward_ref[0, :, c * lanes : (c + 1) * lanes] = from_peer[c]
    for copy in sent:
        copy.wait_send()


def on_device(
    leaf_inverse, leaf_rhs, off_blocks, block_rows, fill_count, sep_rhs, panel_order, sep_inverse
):
    leaves, width = leaf_inverse.shape[:2]
    probes = leaf_rhs.shape[2]
    slots = off_blocks.shape[1]
    fronts = lax.axis_size("front")
    steps = leaves // LEAF_STEP
    block = (width, probes)
    lanes = 128
    chunks = probes // lanes
    piece = (width, lanes)
    lines = fronts // chunks
    rows = block_rows.T
    panel = sep_inverse.reshape(width, fronts * width)
    peer_panels = jnp.stack(
        [
            lax.ppermute(
                panel,
                "front",
                [(i // chunks * chunks + (i + k) % chunks, i) for i in range(fronts)],
            )
            for k in range(1, chunks)
        ]
    )

    smem = pl.BlockSpec(memory_space=pltpu.SMEM)
    vmem = pl.BlockSpec(memory_space=pltpu.VMEM)
    inverse_spec = pl.BlockSpec((LEAF_STEP, width, width), lambda i: (i, 0, 0))
    vector_spec = pl.BlockSpec((LEAF_STEP,) + block, lambda i: (i, 0, 0))
    off_spec = pl.BlockSpec((LEAF_STEP, slots, width, width), lambda i: (i, 0, 0, 0))
    field_spec = pl.BlockSpec((chunks, 2 * fronts) + piece, lambda i: (0, 0, 0, 0))
    one_spec = pl.BlockSpec((1,) + block, lambda i: (0, 0, 0))
    flops = 2 * leaves * (slots + 1) * width * width * probes
    moved = 2 * leaves * width * (width * (slots + 1) + 2 * probes)
    cost = pl.CostEstimate(flops=flops, bytes_accessed=moved, transcendentals=0)

    forward, partial = pl.pallas_call(
        leaf_forward,
        grid=(steps,),
        out_shape=(
            jax.ShapeDtypeStruct((leaves,) + block, BF16),
            jax.ShapeDtypeStruct((chunks, 2 * fronts) + piece, BF16),
        ),
        in_specs=[smem, smem, inverse_spec, vector_spec, off_spec],
        out_specs=(vector_spec, field_spec),
        scratch_shapes=[pltpu.VMEM((2 * fronts + 1,) + block, F32)],
        compiler_params=pltpu.CompilerParams(vmem_limit_bytes=VMEM_BYTES),
        cost_estimate=cost,
        name="leaf_forward",
    )(rows, fill_count, leaf_inverse, leaf_rhs, off_blocks)

    dma = pltpu.SemaphoreType.DMA
    by_line, by_both = dma((lines,)), dma((chunks, lines))
    whole = pltpu.VMEM((chunks, fronts) + piece, BF16)
    part = pltpu.VMEM((fronts,) + piece, BF16)
    small = pltpu.VMEM((chunks,) + piece, BF16)

    field, sep_forward, sep_solution = pl.pallas_call(
        separators,
        out_shape=(
            jax.ShapeDtypeStruct((chunks, 2 * fronts) + piece, BF16),
            jax.ShapeDtypeStruct((1,) + block, BF16),
            jax.ShapeDtypeStruct((1,) + block, F32),
        ),
        in_specs=[smem, vmem, vmem, vmem, vmem],
        out_specs=(vmem, vmem, vmem),
        scratch_shapes=[
            whole, whole, whole, part, part, part, part, part, part, small, small,
            pltpu.VMEM((fronts * width, chunks * width), BF16),
            by_both, by_both, by_both, by_both, by_line, by_line, by_line, by_line,
            by_line, by_line, by_line, by_line, by_line, by_line, by_both, by_both,
            by_both, by_both, dma((chunks,)), dma((chunks,)),
        ],
        compiler_params=pltpu.CompilerParams(
            collective_id=0, has_side_effects=True, vmem_limit_bytes=VMEM_BYTES
        ),
        cost_estimate=pl.CostEstimate(
            flops=4 * fronts * width * width * probes,
            bytes_accessed=8 * fronts * width * probes,
            transcendentals=0,
        ),
        name="separators",
    )(panel_order, partial, sep_rhs, panel, peer_panels)

    return pl.pallas_call(
        leaf_backward,
        grid=(steps,),
        out_shape=(
            jax.ShapeDtypeStruct((leaves,) + block, BF16),
            jax.ShapeDtypeStruct((1,) + block, BF16),
            jax.ShapeDtypeStruct((1,) + block, F32),
        ),
        in_specs=[
            smem, smem, field_spec, inverse_spec, off_spec, vector_spec, one_spec, one_spec,
        ],
        out_specs=(vector_spec, one_spec, one_spec),
        compiler_params=pltpu.CompilerParams(vmem_limit_bytes=VMEM_BYTES),
        cost_estimate=cost,
        name="leaf_backward",
    )(rows, fill_count, field, leaf_inverse, off_blocks, forward, sep_forward, sep_solution)


def solution(mesh):
    placed = (
        P(("leaf", "front"), None, None),
        P(("leaf", "front"), None, None),
        P(("leaf", "front"), None, None, None),
        P(("leaf", "front"), None),
        P(("leaf", "front")),
        P(("leaf", "front"), None, None),
        P("leaf", None),
        P(("leaf", "front"), None, None),
    )
    return jax.shard_map(
        on_device,
        mesh=mesh,
        in_specs=placed,
        out_specs=(
            P(("leaf", "front"), None, None),
            P(("leaf", "front"), None, None),
            P(("leaf", "front"), None, None),
        ),
        check_vma=False,
    )
```

time: 93.4 us -> 76.4 us (0.82)
  the two profiles are of different devices: /device:TPU:0 before, /device:TPU:12 now
where the time goes in v2:
time: 76.4 us; the launch traced here: 75.8 us
  Pallas kernels  72.9 us (95%)
  starting transfers between devices  1.56 us (2%)
    pallas_call x1, Pallas kernels, on_device(): pl.pallas_call(separators, out_shape=(jax.ShapeDtypeStruct((chunks, 2 * f...  49.9 us
    pallas_call x1, Pallas kernels, on_device(): pl.pallas_call(leaf_backward, grid=(steps,), out_shape=(jax.ShapeDtypeStr...  11.8 us
    pallas_call x1, Pallas kernels, on_device(): pl.pallas_call(leaf_forward, grid=(steps,), out_shape=(jax.ShapeDtypeStru...  11.2 us
    ppermute x1, starting transfers between devices, on_device(): lax.ppermute(panel, 'front', [(i // chunks * chunks + (i + k) % chunks, i...  1.56 us
  transfers between devices with their start and end apart: 1, of which 0 were waited for; matrix products, arithmetic and copies ran while one was open for 0% of the time, Pallas kernels for 15%

profile of v2, /device:TPU:12, one launch (start us, length us, event | category | flops | bytes accessed | tf_op | source)
XLA Modules:
  0.0 75.8 jit_solution(1530400870006340535)
XLA Ops:
  0.6 1.6 %collective-permute-start = (bf16[128,1024]{1,0:T(8,128)(2,1)}, bf16[128,1024]{1,0:T(8,128)(2,1)S(1)}, u32[]{:S(2)}, u32[]{:S(2)}) collective-permute-start(bf16[128,1024]{1,0:T(8,128)(2,1)} %bitcast.3), channel_id=1, source_target_pairs={{1,0},{0,1},{3,2},{2,3},{5,4},{4,5},{7,6},{6,7},{9,8},{8,9},{11,10... | collective-permute-start | bytes 786440 | tf_op jit(solution)/shard_map/ppermute | solution.py:291
  2.2 11.2 %leaf_forward.1 = (bf16[32,128,256]{2,1,0:T(8,128)(2,1)}, bf16[2,16,128,128]{3,2,1,0:T(8,128)(2,1)}) custom-call(s32[5,32]{1,0:T(8,128)} %bitcast.6, s32[32]{0:T(128)} %fill_ref.3, bf16[32,128,128]{2,1,0:T(8,128)(2,1)} %inverse_ref.3, bf16[32,128,256]{2,1,0:T(8,128)(2,1)} %rhs_ref.2, bf16[32,5,128,128]{3,2,1,0:T(8,128)(2,1)} %off_ref.3), custom_call_target="tpu_custom_call" | custom-call | flops 1610612736 | bytes 10485760 | tf_op jit(solution)/shard_map/leaf_forward/pallas_call | solution.py:311
  13.4 0.0 collective-permute-done
  13.4 0.0 copy-start
  13.4 0.7 copy-done
  14.1 49.9 %separators.1 = (bf16[2,16,128,128]{3,2,1,0:T(8,128)(2,1)}, bf16[1,128,256]{2,1,0:T(8,128)(2,1)}, f32[1,128,256]{2,1,0:T(8,128)}) custom-call(s32[1,8]{1,0:T(1,128)} %order_ref.1, bf16[2,16,128,128]{3,2,1,0:T(8,128)(2,1)} %get-tuple-element.8.partial_ref, bf16[1,128,256]{2,1,0:T(8,128)(2,1)} %rhs_ref.3, bf16[128,1024]{1,0:T(8,128)(2,1)} %bitcast.4, ...), custom_call_target="tpu_custom_call" | custom-call | flops 134217728 | bytes 2097152 | tf_op jit(solution)/shard_map/separators/pallas_call | solution.py:332
  64.0 11.8 %leaf_backward.1 = (bf16[32,128,256]{2,1,0:T(8,128)(2,1)}, bf16[1,128,256]{2,1,0:T(8,128)(2,1)}, f32[1,128,256]{2,1,0:T(8,128)}) custom-call(s32[5,32]{1,0:T(8,128)} %bitcast.7, s32[32]{0:T(128)} %fill_ref.3, bf16[2,16,128,128]{3,2,1,0:T(8,128)(2,1)} %get-tuple-element.9.field_ref, bf16[32,128,128]{2,1,0:T(8,128)(2,1)} %inverse_ref.3, ...), custom_call_target="tpu_custom_call" | custom-call | flops 1610612736 | bytes 10485760 | tf_op jit(solution)/shard_map/leaf_backward/pallas_call | solution.py:359
Async XLA Ops:
  0.6 12.8 %collective-permute-start = (bf16[128,1024]{1,0:T(8,128)(2,1)}, bf16[128,1024]{1,0:T(8,128)(2,1)S(1)}, u32[]{:S(2)}, u32[]{:S(2)}) collective-permute-start(bf16[128,1024]{1,0:T(8,128)(2,1)} %bitcast.3), channel_id=1, source_target_pairs={{1,0},{0,1},{3,2},{2,3},{5,4},{4,5},{7,6},{6,7},{9,8},{8,9},{11,10... | collective-permute-start | bytes 786440 | tf_op jit(solution)/shard_map/ppermute | solution.py:291
  13.4 0.7 copy-start

commit v3 on v2

--- a/solution.py
+++ b/solution.py
@@ -8,43 +8,51 @@
 MESH = pl.DeviceIdType.MESH
 F32 = jnp.float32
 BF16 = jnp.bfloat16
-LEAF_STEP = 4
+LEAF_STEP = 8
 VMEM_BYTES = 56 * 1024 * 1024
-FIRST_DIMS = (((0,), (0,)), ((), ()))
-
-
-def leaf_forward(rows_ref, fill_ref, inverse_ref, rhs_ref, off_ref, forward_ref, partial_ref, acc):
+
+
+def leaf_forward(
+    rows_ref, fill_ref, inverse_ref, rhs_ref, off_ref, forward_ref, turned_ref, partial_ref, *accs
+):
     step = pl.program_id(0)
     chunks, seps, _, lanes = partial_ref.shape
     slots, width = off_ref.shape[1], off_ref.shape[2]
+    bands = len(accs) // chunks
+    band = width // bands
 
     @pl.when(step == 0)
     def _():
-        acc[...] = jnp.zeros_like(acc)
+        for acc in accs:
+            acc[...] = jnp.zeros_like(acc)
 
     for i in range(LEAF_STEP):
         leaf = step * LEAF_STEP + i
         forward = jnp.dot(inverse_ref[i], rhs_ref[i], preferred_element_type=F32).astype(BF16)
         forward_ref[i] = forward
-        product = jnp.dot(
-            off_ref[i].reshape(slots * width, width), forward, preferred_element_type=F32
-        )
+        stacked = off_ref[i].reshape(slots * width, width)
+        product = jnp.dot(stacked, forward, preferred_element_type=F32)
+        turned_ref[i, :, : slots * width] = stacked.T
+        turned_ref[i, :, slots * width :] = inverse_ref[i].T
         for p in range(slots):
             target = jnp.where(p < fill_ref[leaf], rows_ref[p, leaf], seps)
-            acc[target] += product[p * width : (p + 1) * width]
+            for k, acc in enumerate(accs):
+                c, top = k % chunks, p * width + k // chunks * band
+                acc[target] += product[top : top + band, c * lanes : (c + 1) * lanes]
 
     @pl.when(step == pl.num_programs(0) - 1)
     def _():
-        for c in range(chunks):
-            partial_ref[c] = acc[:seps, :, c * lanes : (c + 1) * lanes].astype(BF16)
+        for k, acc in enumerate(accs):
+            top = k // chunks * band
+            partial_ref[k % chunks, :, top : top + band, :] = acc[:seps].astype(BF16)
 
 
 def leaf_backward(
-    rows_ref, fill_ref, field_ref, inverse_ref, off_ref, forward_ref, sep_fwd_ref, sep_sol_ref,
+    rows_ref, fill_ref, field_ref, turned_ref, forward_ref, sep_fwd_ref, sep_sol_ref,
     out_ref, sep_fwd_out, sep_sol_out,
 ):
     step = pl.program_id(0)
-    slots, width = off_ref.shape[1], off_ref.shape[2]
+    slots, width = rows_ref.shape[0], turned_ref.shape[1]
 
     @pl.when(step == 0)
     def _():
@@ -58,26 +66,25 @@
             row = rows_ref[p, leaf]
             block = jnp.concatenate([field_ref[c, row] for c in range(field_ref.shape[0])], axis=1)
             picked.append(jnp.where(p < fill_ref[leaf], block, jnp.zeros_like(block)))
-        pulled = lax.dot_general(
-            off_ref[i].reshape(slots * width, width),
+        pulled = jnp.dot(
+            turned_ref[i, :, : slots * width],
             jnp.concatenate(picked, axis=0),
-            FIRST_DIMS,
             preferred_element_type=F32,
         )
         backward = (forward_ref[i].astype(F32) - pulled).astype(BF16)
-        out_ref[i] = lax.dot_general(
-            inverse_ref[i], backward, FIRST_DIMS, preferred_element_type=F32
+        out_ref[i] = jnp.dot(
+            turned_ref[i, :, slots * width :], backward, preferred_element_type=F32
         ).astype(BF16)
 
 
 def separators(
-    order_ref, partial_ref, rhs_ref, panel_ref, peer_panel_ref,
+    order_ref, partial_ref, rhs_ref, panel_ref,
     field_ref, forward_ref, solution_ref,
     from_core, to_x, from_x, to_z, from_z, gathered_in, to_adjoint, from_adjoint, gathered_fwd,
-    to_peer, from_peer, panel_t,
+    to_peer, from_peer, panel_t, peer_panel,
     core_send, core_recv, x_send, x_recv, z_send, z_recv, in_send, in_recv, adj_send, adj_recv,
     fwd_send, fwd_recv, sol_send, sol_recv, sol_x_send, sol_x_recv, sib_send, sib_recv,
-    peer_send, peer_recv,
+    peer_send, peer_recv, panel_send, panel_recv,
 ):
     chunks, seps, width, lanes = partial_ref.shape
     fronts = seps // 2
@@ -153,6 +160,8 @@
                 to_x.at[pp, group(ll)], from_x.at[part, group(ll)],
                 x_send.at[pp, ll], x_recv.at[part, ll], across(pp),
             )
+    for pp in parts:
+        push(panel_ref, peer_panel.at[part], panel_send.at[pp], panel_recv.at[part], across(pp))
     totals = []
     for ll in order:
         arrived(from_core.at[part, group(ll)], core_recv.at[part, ll])
@@ -180,7 +189,9 @@
     for ll in others:
         push(gathered_in.at[mine], gathered_in.at[mine], in_send.at[ll], in_recv.at[line], along(ll))
 
-    panels = [panel_ref] + [peer_panel_ref.at[k] for k in range(chunks - 1)]
+    for pp in parts:
+        arrived(peer_panel.at[pp], panel_recv.at[pp])
+    panels = [panel_ref] + [peer_panel.at[pp] for pp in parts]
     for f in range(fronts):
         for k, panel in enumerate(panels):
             panel_t[f * width : (f + 1) * width, k * width : (k + 1) * width] = panel[
@@ -232,14 +243,14 @@
     share_across(line)
     share(part, line)
     for ll in others:
+        arrived(field_ref.at[part, group(ll, base)], sol_recv.at[ll])
+        share_across(ll)
+        share(part, ll)
+    for ll in others:
         push(
             gathered_fwd.at[mine], gathered_fwd.at[mine],
             fwd_send.at[ll], fwd_recv.at[line], along(ll),
         )
-    for ll in others:
-        arrived(field_ref.at[part, group(ll, base)], sol_recv.at[ll])
-        share_across(ll)
-        share(part, ll)
     for ll in [line] + others:
         for pp in parts:
             arrived(field_ref.at[pp, group(ll, base)], sol_x_recv.at[pp, ll])
@@ -286,38 +297,30 @@
     lines = fronts // chunks
     rows = block_rows.T
     panel = sep_inverse.reshape(width, fronts * width)
-    peer_panels = jnp.stack(
-        [
-            lax.ppermute(
-                panel,
-                "front",
-                [(i // chunks * chunks + (i + k) % chunks, i) for i in range(fronts)],
-            )
-            for k in range(1, chunks)
-        ]
-    )
 
     smem = pl.BlockSpec(memory_space=pltpu.SMEM)
     vmem = pl.BlockSpec(memory_space=pltpu.VMEM)
     inverse_spec = pl.BlockSpec((LEAF_STEP, width, width), lambda i: (i, 0, 0))
     vector_spec = pl.BlockSpec((LEAF_STEP,) + block, lambda i: (i, 0, 0))
     off_spec = pl.BlockSpec((LEAF_STEP, slots, width, width), lambda i: (i, 0, 0, 0))
+    turned_spec = pl.BlockSpec((LEAF_STEP, width, (slots + 1) * width), lambda i: (i, 0, 0))
     field_spec = pl.BlockSpec((chunks, 2 * fronts) + piece, lambda i: (0, 0, 0, 0))
     one_spec = pl.BlockSpec((1,) + block, lambda i: (0, 0, 0))
     flops = 2 * leaves * (slots + 1) * width * width * probes
     moved = 2 * leaves * width * (width * (slots + 1) + 2 * probes)
     cost = pl.CostEstimate(flops=flops, bytes_accessed=moved, transcendentals=0)
 
-    forward, partial = pl.pallas_call(
+    forward, turned, partial = pl.pallas_call(
         leaf_forward,
         grid=(steps,),
         out_shape=(
             jax.ShapeDtypeStruct((leaves,) + block, BF16),
+            jax.ShapeDtypeStruct((leaves, width, (slots + 1) * width), BF16),
             jax.ShapeDtypeStruct((chunks, 2 * fronts) + piece, BF16),
         ),
         in_specs=[smem, smem, inverse_spec, vector_spec, off_spec],
-        out_specs=(vector_spec, field_spec),
-        scratch_shapes=[pltpu.VMEM((2 * fronts + 1,) + block, F32)],
+        out_specs=(vector_spec, turned_spec, field_spec),
+        scratch_shapes=[pltpu.VMEM((2 * fronts + 1, width // 2, lanes), F32)] * (2 * chunks),
         compiler_params=pltpu.CompilerParams(vmem_limit_bytes=VMEM_BYTES),
         cost_estimate=cost,
         name="leaf_forward",
@@ -336,14 +339,15 @@
             jax.ShapeDtypeStruct((1,) + block, BF16),
             jax.ShapeDtypeStruct((1,) + block, F32),
         ),
-        in_specs=[smem, vmem, vmem, vmem, vmem],
+        in_specs=[smem, vmem, vmem, vmem],
         out_specs=(vmem, vmem, vmem),
         scratch_shapes=[
             whole, whole, whole, part, part, part, part, part, part, small, small,
             pltpu.VMEM((fronts * width, chunks * width), BF16),
+            pltpu.VMEM((chunks, width, fronts * width), BF16),
             by_both, by_both, by_both, by_both, by_line, by_line, by_line, by_line,
             by_line, by_line, by_line, by_line, by_line, by_line, by_both, by_both,
-            by_both, by_both, dma((chunks,)), dma((chunks,)),
+            by_both, by_both, dma((chunks,)), dma((chunks,)), dma((chunks,)), dma((chunks,)),
         ],
         compiler_params=pltpu.CompilerParams(
             collective_id=0, has_side_effects=True, vmem_limit_bytes=VMEM_BYTES
@@ -354,7 +358,7 @@
             transcendentals=0,
         ),
         name="separators",
-    )(panel_order, partial, sep_rhs, panel, peer_panels)
+    )(panel_order, partial, sep_rhs, panel)
 
     return pl.pallas_call(
         leaf_backward,
@@ -365,13 +369,13 @@
             jax.ShapeDtypeStruct((1,) + block, F32),
         ),
         in_specs=[
-            smem, smem, field_spec, inverse_spec, off_spec, vector_spec, one_spec, one_spec,
+            smem, smem, field_spec, turned_spec, vector_spec, one_spec, one_spec,
         ],
         out_specs=(vector_spec, one_spec, one_spec),
         compiler_params=pltpu.CompilerParams(vmem_limit_bytes=VMEM_BYTES),
         cost_estimate=cost,
         name="leaf_backward",
-    )(rows, fill_count, field, leaf_inverse, off_blocks, forward, sep_forward, sep_solution)
+    )(rows, fill_count, field, turned, forward, sep_forward, sep_solution)
 
 
 def solution(mesh):

time: 76.4 us -> 72.7 us (0.952)
  the two profiles are of different devices: /device:TPU:12 before, /device:TPU:0 now
where the time goes in v3:
time: 72.7 us; the launch traced here: 72.5 us
  Pallas kernels  71.9 us (99%)
    pallas_call x1, Pallas kernels, on_device(): pl.pallas_call(separators, out_shape=(jax.ShapeDtypeStruct((chunks, 2 * f...  50 us
    pallas_call x1, Pallas kernels, on_device(): pl.pallas_call(leaf_backward, grid=(steps,), out_shape=(jax.ShapeDtypeStr...  11 us
    pallas_call x1, Pallas kernels, on_device(): pl.pallas_call(leaf_forward, grid=(steps,), out_shape=(jax.ShapeDtypeStru...  10.8 us

profile of v3, /device:TPU:0, one launch (start us, length us, event | category | flops | bytes accessed | tf_op | source)
XLA Modules:
  0.0 72.5 jit_solution(10554879315415244533)
XLA Ops:
  0.6 10.8 %leaf_forward.1 = (bf16[32,128,256]{2,1,0:T(8,128)(2,1)}, bf16[32,128,768]{2,1,0:T(8,128)(2,1)}, bf16[2,16,128,128]{3,2,1,0:T(8,128)(2,1)}) custom-call(s32[5,32]{1,0:T(8,128)} %bitcast.3, s32[32]{0:T(128)} %fill_ref.3, bf16[32,128,128]{2,1,0:T(8,128)(2,1)} %inverse_ref.1, bf16[32,128,256]{2,1,0:T(8,128)(2,1)} %rhs_ref.2, bf16[32,5,128,128]{3,2,1,0:T(8,128)(2,1)} %off_ref.1), custom_call_target="tpu_custom_call" | custom-call | flops 1610612736 | bytes 10485760 | tf_op jit(solution)/shard_map/leaf_forward/pallas_call | solution.py:313
  11.5 50.0 %separators.1 = (bf16[2,16,128,128]{3,2,1,0:T(8,128)(2,1)}, bf16[1,128,256]{2,1,0:T(8,128)(2,1)}, f32[1,128,256]{2,1,0:T(8,128)}) custom-call(s32[1,8]{1,0:T(1,128)} %order_ref.1, bf16[2,16,128,128]{3,2,1,0:T(8,128)(2,1)} %get-tuple-element.9.partial_ref, bf16[1,128,256]{2,1,0:T(8,128)(2,1)} %rhs_ref.3, bf16[128,1024]{1,0:T(8,128)(2,1)} %bitcast.2), custom_call_target="tpu_custom_call" | custom-call | flops 134217728 | bytes 2097152 | tf_op jit(solution)/shard_map/separators/pallas_call | solution.py:335
  61.5 11.0 %leaf_backward.1 = (bf16[32,128,256]{2,1,0:T(8,128)(2,1)}, bf16[1,128,256]{2,1,0:T(8,128)(2,1)}, f32[1,128,256]{2,1,0:T(8,128)}) custom-call(s32[5,32]{1,0:T(8,128)} %bitcast.4, s32[32]{0:T(128)} %fill_ref.3, bf16[2,16,128,128]{3,2,1,0:T(8,128)(2,1)} %get-tuple-element.10.field_ref, bf16[32,128,768]{2,1,0:T(8,128)(2,1)} %get-tuple-element.11.turned_ref, ...), custom_call_target="tpu_custom_call" | custom-call | flops 1610612736 | bytes 10485760 | tf_op jit(solution)/shard_map/leaf_backward/pallas_call | solution.py:363

commit v4 on v3

--- a/solution.py
+++ b/solution.py
@@ -27,11 +27,13 @@
             acc[...] = jnp.zeros_like(acc)
 
     for i in range(LEAF_STEP):
+        forward_ref[i] = jnp.dot(
+            inverse_ref[i], rhs_ref[i], preferred_element_type=F32
+        ).astype(BF16)
+    for i in range(LEAF_STEP):
         leaf = step * LEAF_STEP + i
-        forward = jnp.dot(inverse_ref[i], rhs_ref[i], preferred_element_type=F32).astype(BF16)
-        forward_ref[i] = forward
         stacked = off_ref[i].reshape(slots * width, width)
-        product = jnp.dot(stacked, forward, preferred_element_type=F32)
+        product = jnp.dot(stacked, forward_ref[i], preferred_element_type=F32)
         turned_ref[i, :, : slots * width] = stacked.T
         turned_ref[i, :, slots * width :] = inverse_ref[i].T
         for p in range(slots):
@@ -49,7 +51,7 @@
 
 def leaf_backward(
     rows_ref, fill_ref, field_ref, turned_ref, forward_ref, sep_fwd_ref, sep_sol_ref,
-    out_ref, sep_fwd_out, sep_sol_out,
+    out_ref, sep_fwd_out, sep_sol_out, backward,
 ):
     step = pl.program_id(0)
     slots, width = rows_ref.shape[0], turned_ref.shape[1]
@@ -71,9 +73,10 @@
             jnp.concatenate(picked, axis=0),
             preferred_element_type=F32,
         )
-        backward = (forward_ref[i].astype(F32) - pulled).astype(BF16)
+        backward[i] = (forward_ref[i].astype(F32) - pulled).astype(BF16)
+    for i in range(LEAF_STEP):
         out_ref[i] = jnp.dot(
-            turned_ref[i, :, slots * width :], backward, preferred_element_type=F32
+            turned_ref[i, :, slots * width :], backward[i], preferred_element_type=F32
         ).astype(BF16)
 
 
@@ -243,14 +246,14 @@
     share_across(line)
     share(part, line)
     for ll in others:
-        arrived(field_ref.at[part, group(ll, base)], sol_recv.at[ll])
-        share_across(ll)
-        share(part, ll)
-    for ll in others:
         push(
             gathered_fwd.at[mine], gathered_fwd.at[mine],
             fwd_send.at[ll], fwd_recv.at[line], along(ll),
         )
+    for ll in others:
+        arrived(field_ref.at[part, group(ll, base)], sol_recv.at[ll])
+        share_across(ll)
+        share(part, ll)
     for ll in [line] + others:
         for pp in parts:
             arrived(field_ref.at[pp, group(ll, base)], sol_x_recv.at[pp, ll])
@@ -372,6 +375,7 @@
             smem, smem, field_spec, turned_spec, vector_spec, one_spec, one_spec,
         ],
         out_specs=(vector_spec, one_spec, one_spec),
+        scratch_shapes=[pltpu.VMEM((LEAF_STEP,) + block, BF16)],
         compiler_params=pltpu.CompilerParams(vmem_limit_bytes=VMEM_BYTES),
         cost_estimate=cost,
         name="leaf_backward",

time: 72.7 us -> 68.7 us (0.945); the launches traced: 72.5 us -> 67.5 us
  Pallas kernels: 71.9 us -> 66.9 us
    pallas_call x1, Pallas kernels: 11 us -> 7.03 us  [on_device(): pl.pallas_call(leaf_backward, grid=(steps,), out_shape=(jax.ShapeDtypeStr...]
    pallas_call x1, Pallas kernels: 10.8 us -> 9.78 us  [on_device(): pl.pallas_call(leaf_forward, grid=(steps,), out_shape=(jax.ShapeDtypeStru...]
where the time goes in v4:
time: 68.7 us; the launch traced here: 67.5 us
  Pallas kernels  66.9 us (97%)
    pallas_call x1, Pallas kernels, on_device(): pl.pallas_call(separators, out_shape=(jax.ShapeDtypeStruct((chunks, 2 * f...  50.1 us
    pallas_call x1, Pallas kernels, on_device(): pl.pallas_call(leaf_forward, grid=(steps,), out_shape=(jax.ShapeDtypeStru...  9.78 us
    pallas_call x1, Pallas kernels, on_device(): pl.pallas_call(leaf_backward, grid=(steps,), out_shape=(jax.ShapeDtypeStr...  7.03 us

profile of v4, /device:TPU:0, one launch (start us, length us, event | category | flops | bytes accessed | tf_op | source)
XLA Modules:
  0.0 67.5 jit_solution(9658016939798812870)
XLA Ops:
  0.6 9.8 %leaf_forward.1 = (bf16[32,128,256]{2,1,0:T(8,128)(2,1)}, bf16[32,128,768]{2,1,0:T(8,128)(2,1)}, bf16[2,16,128,128]{3,2,1,0:T(8,128)(2,1)}) custom-call(s32[5,32]{1,0:T(8,128)} %bitcast.3, s32[32]{0:T(128)} %fill_ref.3, bf16[32,128,128]{2,1,0:T(8,128)(2,1)} %inverse_ref.1, bf16[32,128,256]{2,1,0:T(8,128)(2,1)} %rhs_ref.2, bf16[32,5,128,128]{3,2,1,0:T(8,128)(2,1)} %off_ref.1), custom_call_target="tpu_custom_call" | custom-call | flops 1610612736 | bytes 10485760 | tf_op jit(solution)/shard_map/leaf_forward/pallas_call | solution.py:316
  10.4 50.1 %separators.1 = (bf16[2,16,128,128]{3,2,1,0:T(8,128)(2,1)}, bf16[1,128,256]{2,1,0:T(8,128)(2,1)}, f32[1,128,256]{2,1,0:T(8,128)}) custom-call(s32[1,8]{1,0:T(1,128)} %order_ref.1, bf16[2,16,128,128]{3,2,1,0:T(8,128)(2,1)} %get-tuple-element.9.partial_ref, bf16[1,128,256]{2,1,0:T(8,128)(2,1)} %rhs_ref.3, bf16[128,1024]{1,0:T(8,128)(2,1)} %bitcast.2), custom_call_target="tpu_custom_call" | custom-call | flops 134217728 | bytes 2097152 | tf_op jit(solution)/shard_map/separators/pallas_call | solution.py:338
  60.5 7.0 %leaf_backward.1 = (bf16[32,128,256]{2,1,0:T(8,128)(2,1)}, bf16[1,128,256]{2,1,0:T(8,128)(2,1)}, f32[1,128,256]{2,1,0:T(8,128)}) custom-call(s32[5,32]{1,0:T(8,128)} %bitcast.4, s32[32]{0:T(128)} %fill_ref.3, bf16[2,16,128,128]{3,2,1,0:T(8,128)(2,1)} %get-tuple-element.10.field_ref, bf16[32,128,768]{2,1,0:T(8,128)(2,1)} %get-tuple-element.11.turned_ref, ...), custom_call_target="tpu_custom_call" | custom-call | flops 1610612736 | bytes 10485760 | tf_op jit(solution)/shard_map/leaf_backward/pallas_call | solution.py:366

commit v5 on v3

--- a/solution.py
+++ b/solution.py
@@ -27,11 +27,13 @@
             acc[...] = jnp.zeros_like(acc)
 
     for i in range(LEAF_STEP):
+        forward_ref[i] = jnp.dot(
+            inverse_ref[i], rhs_ref[i], preferred_element_type=F32
+        ).astype(BF16)
+    for i in range(LEAF_STEP):
         leaf = step * LEAF_STEP + i
-        forward = jnp.dot(inverse_ref[i], rhs_ref[i], preferred_element_type=F32).astype(BF16)
-        forward_ref[i] = forward
         stacked = off_ref[i].reshape(slots * width, width)
-        product = jnp.dot(stacked, forward, preferred_element_type=F32)
+        product = jnp.dot(stacked, forward_ref[i], preferred_element_type=F32)
         turned_ref[i, :, : slots * width] = stacked.T
         turned_ref[i, :, slots * width :] = inverse_ref[i].T
         for p in range(slots):
@@ -47,46 +49,24 @@
             partial_ref[k % chunks, :, top : top + band, :] = acc[:seps].astype(BF16)
 
 
-def leaf_backward(
-    rows_ref, fill_ref, field_ref, turned_ref, forward_ref, sep_fwd_ref, sep_sol_ref,
-    out_ref, sep_fwd_out, sep_sol_out,
-):
-    step = pl.program_id(0)
-    slots, width = rows_ref.shape[0], turned_ref.shape[1]
-
-    @pl.when(step == 0)
-    def _():
-        sep_fwd_out[...] = sep_fwd_ref[...]
-        sep_sol_out[...] = sep_sol_ref[...]
-
-    for i in range(LEAF_STEP):
-        leaf = step * LEAF_STEP + i
-        picked = []
-        for p in range(slots):
-            row = rows_ref[p, leaf]
-            block = jnp.concatenate([field_ref[c, row] for c in range(field_ref.shape[0])], axis=1)
-            picked.append(jnp.where(p < fill_ref[leaf], block, jnp.zeros_like(block)))
-        pulled = jnp.dot(
-            turned_ref[i, :, : slots * width],
-            jnp.concatenate(picked, axis=0),
-            preferred_element_type=F32,
-        )
-        backward = (forward_ref[i].astype(F32) - pulled).astype(BF16)
-        out_ref[i] = jnp.dot(
-            turned_ref[i, :, slots * width :], backward, preferred_element_type=F32
-        ).astype(BF16)
-
-
 def separators(
-    order_ref, partial_ref, rhs_ref, panel_ref,
-    field_ref, forward_ref, solution_ref,
+    rows_ref, fill_ref, order_ref, partial_ref, rhs_ref, panel_ref, turned_hbm, leaf_forward_hbm,
+    leaf_hbm, forward_ref, solution_ref,
+    turned_ref, leaf_forward_ref, backward, leaf_out, load_sems, store_sems, field_ref,
     from_core, to_x, from_x, to_z, from_z, gathered_in, to_adjoint, from_adjoint, gathered_fwd,
     to_peer, from_peer, panel_t, peer_panel,
     core_send, core_recv, x_send, x_recv, z_send, z_recv, in_send, in_recv, adj_send, adj_recv,
     fwd_send, fwd_recv, sol_send, sol_recv, sol_x_send, sol_x_recv, sib_send, sib_recv,
     peer_send, peer_recv, panel_send, panel_recv,
 ):
+    loads = [
+        pltpu.make_async_copy(turned_hbm, turned_ref, load_sems.at[0]),
+        pltpu.make_async_copy(leaf_forward_hbm, leaf_forward_ref, load_sems.at[1]),
+    ]
+    for load in loads:
+        load.start()
     chunks, seps, width, lanes = partial_ref.shape
+    slots = rows_ref.shape[0]
     fronts = seps // 2
     lines = fronts // chunks
     leaf, me = lax.axis_index("leaf"), lax.axis_index("front")
@@ -258,6 +238,41 @@
     for c in range(chunks):
         solution_ref[0, :, c * lanes : (c + 1) * lanes] = field_ref[c, base + me].astype(F32)
 
+    for pp in parts + [part]:
+        for ll in [line] + others:
+            arrived(field_ref.at[pp, group(ll, far_base)], sib_recv.at[pp, ll])
+    for load in loads:
+        load.wait()
+
+    def leaf_store(step):
+        some = pl.ds(step * LEAF_STEP, LEAF_STEP)
+        return pltpu.make_async_copy(leaf_out.at[some], leaf_hbm.at[some], store_sems.at[step])
+
+    def leaf_step(step, carry):
+        for i in range(LEAF_STEP):
+            leaf = step * LEAF_STEP + i
+            picked = []
+            for p in range(slots):
+                row = rows_ref[p, leaf]
+                block = jnp.concatenate([field_ref[c, row] for c in range(chunks)], axis=1)
+                picked.append(jnp.where(p < fill_ref[leaf], block, jnp.zeros_like(block)))
+            pulled = jnp.dot(
+                turned_ref[leaf, :, : slots * width],
+                jnp.concatenate(picked, axis=0),
+                preferred_element_type=F32,
+            )
+            backward[i] = (leaf_forward_ref[leaf].astype(F32) - pulled).astype(BF16)
+        for i in range(LEAF_STEP):
+            leaf = step * LEAF_STEP + i
+            leaf_out[leaf] = jnp.dot(
+                turned_ref[leaf, :, slots * width :], backward[i], preferred_element_type=F32
+            ).astype(BF16)
+        leaf_store(step).start()
+        return carry
+
+    steps = leaf_out.shape[0] // LEAF_STEP
+    lax.fori_loop(0, steps // 2, leaf_step, 0)
+
     for ll in others:
         arrived(gathered_fwd.at[group(ll)], fwd_recv.at[ll])
 
@@ -271,13 +286,13 @@
     for pp in parts:
         to_peer[pp] = forward_of(line * chunks + pp)
         push(to_peer.at[pp], from_peer.at[part], peer_send.at[pp], peer_recv.at[part], across(pp))
-    for pp in parts + [part]:
-        for ll in [line] + others:
-            arrived(field_ref.at[pp, group(ll, far_base)], sib_recv.at[pp, ll])
+    lax.fori_loop(steps // 2, steps, leaf_step, 0)
     for pp in parts:
         arrived(from_peer.at[pp], peer_recv.at[pp])
     for c in range(chunks):
         forward_ref[0, :, c * lanes : (c + 1) * lanes] = from_peer[c]
+    for step in range(steps):
+        leaf_store(step).wait()
     for copy in sent:
         copy.wait_send()
 
@@ -300,12 +315,12 @@
 
     smem = pl.BlockSpec(memory_space=pltpu.SMEM)
     vmem = pl.BlockSpec(memory_space=pltpu.VMEM)
+    hbm = pl.BlockSpec(memory_space=pl.ANY)
     inverse_spec = pl.BlockSpec((LEAF_STEP, width, width), lambda i: (i, 0, 0))
     vector_spec = pl.BlockSpec((LEAF_STEP,) + block, lambda i: (i, 0, 0))
     off_spec = pl.BlockSpec((LEAF_STEP, slots, width, width), lambda i: (i, 0, 0, 0))
     turned_spec = pl.BlockSpec((LEAF_STEP, width, (slots + 1) * width), lambda i: (i, 0, 0))
     field_spec = pl.BlockSpec((chunks, 2 * fronts) + piece, lambda i: (0, 0, 0, 0))
-    one_spec = pl.BlockSpec((1,) + block, lambda i: (0, 0, 0))
     flops = 2 * leaves * (slots + 1) * width * width * probes
     moved = 2 * leaves * width * (width * (slots + 1) + 2 * probes)
     cost = pl.CostEstimate(flops=flops, bytes_accessed=moved, transcendentals=0)
@@ -332,16 +347,22 @@
     part = pltpu.VMEM((fronts,) + piece, BF16)
     small = pltpu.VMEM((chunks,) + piece, BF16)
 
-    field, sep_forward, sep_solution = pl.pallas_call(
+    leaf_solution, sep_forward, sep_solution = pl.pallas_call(
         separators,
         out_shape=(
-            jax.ShapeDtypeStruct((chunks, 2 * fronts) + piece, BF16),
+            jax.ShapeDtypeStruct((leaves,) + block, BF16),
             jax.ShapeDtypeStruct((1,) + block, BF16),
             jax.ShapeDtypeStruct((1,) + block, F32),
         ),
-        in_specs=[smem, vmem, vmem, vmem],
-        out_specs=(vmem, vmem, vmem),
+        in_specs=[smem, smem, smem, vmem, vmem, vmem, hbm, hbm],
+        out_specs=(hbm, vmem, vmem),
         scratch_shapes=[
+            pltpu.VMEM((leaves, width, (slots + 1) * width), BF16),
+            pltpu.VMEM((leaves,) + block, BF16),
+            pltpu.VMEM((LEAF_STEP,) + block, BF16),
+            pltpu.VMEM((leaves,) + block, BF16),
+            dma((2,)), dma((steps,)),
+            pltpu.VMEM((chunks, 2 * fronts) + piece, BF16),
             whole, whole, whole, part, part, part, part, part, part, small, small,
             pltpu.VMEM((fronts * width, chunks * width), BF16),
             pltpu.VMEM((chunks, width, fronts * width), BF16),
@@ -352,30 +373,10 @@
         compiler_params=pltpu.CompilerParams(
             collective_id=0, has_side_effects=True, vmem_limit_bytes=VMEM_BYTES
         ),
-        cost_estimate=pl.CostEstimate(
-            flops=4 * fronts * width * width * probes,
-            bytes_accessed=8 * fronts * width * probes,
-            transcendentals=0,
-        ),
+        cost_estimate=cost,
         name="separators",
-    )(panel_order, partial, sep_rhs, panel)
-
-    return pl.pallas_call(
-        leaf_backward,
-        grid=(steps,),
-        out_shape=(
-            jax.ShapeDtypeStruct((leaves,) + block, BF16),
-            jax.ShapeDtypeStruct((1,) + block, BF16),
-            jax.ShapeDtypeStruct((1,) + block, F32),
-        ),
-        in_specs=[
-            smem, smem, field_spec, turned_spec, vector_spec, one_spec, one_spec,
-        ],
-        out_specs=(vector_spec, one_spec, one_spec),
-        compiler_params=pltpu.CompilerParams(vmem_limit_bytes=VMEM_BYTES),
-        cost_estimate=cost,
-        name="leaf_backward",
-    )(rows, fill_count, field, turned, forward, sep_forward, sep_solution)
+    )(rows, fill_count, panel_order, partial, sep_rhs, panel, turned, forward)
+    return (leaf_solution, sep_forward, sep_solution)
 
 
 def solution(mesh):

time: 72.7 us -> 66.6 us (0.916)
  the two profiles are of different devices: /device:TPU:0 before, /device:TPU:13 now
where the time goes in v5:
time: 66.6 us; the launch traced here: 66.4 us
  Pallas kernels  61.3 us (92%)
  local copies, waits for them, and re-layouts  4.46 us (7%)
    pallas_call x1, Pallas kernels, on_device(): pl.pallas_call(separators, out_shape=(jax.ShapeDtypeStruct((leaves,) + bl...  51.4 us
    pallas_call x1, Pallas kernels, on_device(): pl.pallas_call(leaf_forward, grid=(steps,), out_shape=(jax.ShapeDtypeStru...  9.86 us
    unnamed x7, local copies, waits for them, and re-layouts  4.46 us

profile of v5, /device:TPU:13, one launch (start us, length us, event | category | flops | bytes accessed | tf_op | source)
XLA Modules:
  0.0 66.4 jit_solution(9467965452629775400)
XLA Ops:
  0.6 9.9 %leaf_forward.1 = (bf16[32,128,256]{2,1,0:T(8,128)(2,1)}, bf16[32,128,768]{2,1,0:T(8,128)(2,1)}, bf16[2,16,128,128]{3,2,1,0:T(8,128)(2,1)}) custom-call(s32[5,32]{1,0:T(8,128)} %bitcast.3, s32[32]{0:T(128)} %fill_ref.3, bf16[32,128,128]{2,1,0:T(8,128)(2,1)} %inverse_ref.1, bf16[32,128,256]{2,1,0:T(8,128)(2,1)} %rhs_ref.2, bf16[32,5,128,128]{3,2,1,0:T(8,128)(2,1)} %off_ref.1), custom_call_target="tpu_custom_call" | custom-call | flops 1610612736 | bytes 10485760 | tf_op jit(solution)/shard_map/leaf_forward/pallas_call | solution.py:328
  10.5 51.4 %separators.1 = (bf16[32,128,256]{2,1,0:T(8,128)(2,1)}, bf16[1,128,256]{2,1,0:T(8,128)(2,1)}, f32[1,128,256]{2,1,0:T(8,128)}) custom-call(s32[5,32]{1,0:T(8,128)} %bitcast.4, s32[32]{0:T(128)} %fill_ref.3, s32[1,8]{1,0:T(1,128)} %order_ref.1, bf16[2,16,128,128]{3,2,1,0:T(8,128)(2,1)} %get-tuple-element.6.partial_ref, bf16[1,128,256]{2,1,0:T(8,128)(2,1)} %rhs_ref.3, ...), custom_call_target="tpu_custom_call" | custom-call | flops 1610612736 | bytes 10485760 | tf_op jit(solution)/shard_map/separators/pallas_call | solution.py:350
  61.9 0.0 copy-start.1
  62.0 0.0 copy-start
  62.0 3.2 %copy.14 = bf16[32,128,256]{2,1,0:T(8,128)(2,1)} copy(bf16[32,128,256]{2,1,0:T(8,128)(2,1)} %get-tuple-element.12) | data formatting | bytes 4194304
  65.1 0.0 copy-done.1
  65.1 0.6 copy.15
  65.8 0.0 copy-done
  65.8 0.7 copy.16
Async XLA Ops:
  61.9 3.2 %copy-start.1 = (bf16[1,128,256]{2,1,0:T(8,128)(2,1)S(1)}, bf16[1,128,256]{2,1,0:T(8,128)(2,1)}, u32[]{:S(2)}) copy-start(bf16[1,128,256]{2,1,0:T(8,128)(2,1)} %get-tuple-element.13) | copy-start | bytes 196612
  62.0 3.8 %copy-start = (f32[1,128,256]{2,1,0:T(8,128)S(1)}, f32[1,128,256]{2,1,0:T(8,128)}, u32[]{:S(2)}) copy-start(f32[1,128,256]{2,1,0:T(8,128)} %get-tuple-element.14) | copy-start | bytes 393220

commit v6 on v5

--- a/solution.py
+++ b/solution.py
@@ -9,11 +9,12 @@
 F32 = jnp.float32
 BF16 = jnp.bfloat16
 LEAF_STEP = 8
+FIRST_DIMS = (((0,), (0,)), ((), ()))
 VMEM_BYTES = 56 * 1024 * 1024
 
 
 def leaf_forward(
-    rows_ref, fill_ref, inverse_ref, rhs_ref, off_ref, forward_ref, turned_ref, partial_ref, *accs
+    rows_ref, fill_ref, inverse_ref, rhs_ref, off_ref, forward_ref, partial_ref, *accs
 ):
     step = pl.program_id(0)
     chunks, seps, _, lanes = partial_ref.shape
@@ -34,8 +35,6 @@
         leaf = step * LEAF_STEP + i
         stacked = off_ref[i].reshape(slots * width, width)
         product = jnp.dot(stacked, forward_ref[i], preferred_element_type=F32)
-        turned_ref[i, :, : slots * width] = stacked.T
-        turned_ref[i, :, slots * width :] = inverse_ref[i].T
         for p in range(slots):
             target = jnp.where(p < fill_ref[leaf], rows_ref[p, leaf], seps)
             for k, acc in enumerate(accs):
@@ -49,10 +48,24 @@
             partial_ref[k % chunks, :, top : top + band, :] = acc[:seps].astype(BF16)
 
 
+def leaf_finish(
+    inverse_ref, backward_ref, sep_fwd_ref, sep_sol_ref, out_ref, sep_fwd_out, sep_sol_out
+):
+    @pl.when(pl.program_id(0) == 0)
+    def _():
+        sep_fwd_out[...] = sep_fwd_ref[...]
+        sep_sol_out[...] = sep_sol_ref[...]
+
+    for i in range(LEAF_STEP):
+        out_ref[i] = lax.dot_general(
+            inverse_ref[i], backward_ref[i], FIRST_DIMS, preferred_element_type=F32
+        ).astype(BF16)
+
+
 def separators(
-    rows_ref, fill_ref, order_ref, partial_ref, rhs_ref, panel_ref, turned_hbm, leaf_forward_hbm,
+    rows_ref, fill_ref, order_ref, partial_ref, rhs_ref, panel_ref, off_hbm, leaf_forward_hbm,
     leaf_hbm, forward_ref, solution_ref,
-    turned_ref, leaf_forward_ref, backward, leaf_out, load_sems, store_sems, field_ref,
+    off_ref, turned_ref, leaf_forward_ref, leaf_out, load_sems, store_sems, field_ref,
     from_core, to_x, from_x, to_z, from_z, gathered_in, to_adjoint, from_adjoint, gathered_fwd,
     to_peer, from_peer, panel_t, peer_panel,
     core_send, core_recv, x_send, x_recv, z_send, z_recv, in_send, in_recv, adj_send, adj_recv,
@@ -60,7 +73,7 @@
     peer_send, peer_recv, panel_send, panel_recv,
 ):
     loads = [
-        pltpu.make_async_copy(turned_hbm, turned_ref, load_sems.at[0]),
+        pltpu.make_async_copy(off_hbm, off_ref, load_sems.at[0]),
         pltpu.make_async_copy(leaf_forward_hbm, leaf_forward_ref, load_sems.at[1]),
     ]
     for load in loads:
@@ -117,6 +130,13 @@
             value = jnp.where(pp == c, rhs[c], value)
         return value
 
+    def turn(step, count=1):
+        def one(leaf, carry):
+            turned_ref[leaf] = off_ref[leaf].reshape(slots * width, width).T
+            return carry
+
+        lax.fori_loop(step * LEAF_STEP, (step + count) * LEAF_STEP, one, 0)
+
     for pp in parts + [part]:
         for ll in order:
             push(
@@ -142,6 +162,8 @@
             )
     for pp in parts:
         push(panel_ref, peer_panel.at[part], panel_send.at[pp], panel_recv.at[part], across(pp))
+    loads[0].wait()
+    turn(0)
     totals = []
     for ll in order:
         arrived(from_core.at[part, group(ll)], core_recv.at[part, ll])
@@ -158,6 +180,7 @@
                 to_z[f] = value.astype(BF16)
         if ll is not line:
             push(to_z.at[group(ll)], from_z.at[group(line)], z_send.at[ll], z_recv.at[line], along(ll))
+    turn(1)
     for ll in others:
         arrived(from_z.at[group(ll)], z_recv.at[ll])
         for k in range(chunks):
@@ -178,6 +201,7 @@
                 :, f * width : (f + 1) * width
             ].T
 
+    turn(2)
     forward = [jnp.zeros((width, lanes), F32)] * chunks
     for ll in [line] + others:
         if ll is not line:
@@ -203,6 +227,8 @@
                 to_adjoint.at[group(ll)], from_adjoint.at[mine],
                 adj_send.at[ll], adj_recv.at[line], along(ll),
             )
+    steps = leaf_out.shape[0] // LEAF_STEP
+    turn(3, steps - 3)
     for ll in others:
         arrived(from_adjoint.at[group(ll)], adj_recv.at[ll])
         solved += from_adjoint[group(ll)].reshape(chunks * width, lanes).astype(F32)
@@ -241,8 +267,7 @@
     for pp in parts + [part]:
         for ll in [line] + others:
             arrived(field_ref.at[pp, group(ll, far_base)], sib_recv.at[pp, ll])
-    for load in loads:
-        load.wait()
+    loads[1].wait()
 
     def leaf_store(step):
         some = pl.ds(step * LEAF_STEP, LEAF_STEP)
@@ -257,20 +282,14 @@
                 block = jnp.concatenate([field_ref[c, row] for c in range(chunks)], axis=1)
                 picked.append(jnp.where(p < fill_ref[leaf], block, jnp.zeros_like(block)))
             pulled = jnp.dot(
-                turned_ref[leaf, :, : slots * width],
+                turned_ref[leaf],
                 jnp.concatenate(picked, axis=0),
                 preferred_element_type=F32,
             )
-            backward[i] = (leaf_forward_ref[leaf].astype(F32) - pulled).astype(BF16)
-        for i in range(LEAF_STEP):
-            leaf = step * LEAF_STEP + i
-            leaf_out[leaf] = jnp.dot(
-                turned_ref[leaf, :, slots * width :], backward[i], preferred_element_type=F32
-            ).astype(BF16)
+            leaf_out[leaf] = (leaf_forward_ref[leaf].astype(F32) - pulled).astype(BF16)
         leaf_store(step).start()
         return carry
 
-    steps = leaf_out.shape[0] // LEAF_STEP
     lax.fori_loop(0, steps // 2, leaf_step, 0)
 
     for ll in others:
@@ -319,22 +338,20 @@
     inverse_spec = pl.BlockSpec((LEAF_STEP, width, width), lambda i: (i, 0, 0))
     vector_spec = pl.BlockSpec((LEAF_STEP,) + block, lambda i: (i, 0, 0))
     off_spec = pl.BlockSpec((LEAF_STEP, slots, width, width), lambda i: (i, 0, 0, 0))
-    turned_spec = pl.BlockSpec((LEAF_STEP, width, (slots + 1) * width), lambda i: (i, 0, 0))
     field_spec = pl.BlockSpec((chunks, 2 * fronts) + piece, lambda i: (0, 0, 0, 0))
     flops = 2 * leaves * (slots + 1) * width * width * probes
     moved = 2 * leaves * width * (width * (slots + 1) + 2 * probes)
     cost = pl.CostEstimate(flops=flops, bytes_accessed=moved, transcendentals=0)
 
-    forward, turned, partial = pl.pallas_call(
+    forward, partial = pl.pallas_call(
         leaf_forward,
         grid=(steps,),
         out_shape=(
             jax.ShapeDtypeStruct((leaves,) + block, BF16),
-            jax.ShapeDtypeStruct((leaves, width, (slots + 1) * width), BF16),
             jax.ShapeDtypeStruct((chunks, 2 * fronts) + piece, BF16),
         ),
         in_specs=[smem, smem, inverse_spec, vector_spec, off_spec],
-        out_specs=(vector_spec, turned_spec, field_spec),
+        out_specs=(vector_spec, field_spec),
         scratch_shapes=[pltpu.VMEM((2 * fronts + 1, width // 2, lanes), F32)] * (2 * chunks),
         compiler_params=pltpu.CompilerParams(vmem_limit_bytes=VMEM_BYTES),
         cost_estimate=cost,
@@ -347,7 +364,7 @@
     part = pltpu.VMEM((fronts,) + piece, BF16)
     small = pltpu.VMEM((chunks,) + piece, BF16)
 
-    leaf_solution, sep_forward, sep_solution = pl.pallas_call(
+    backward, sep_forward, sep_solution = pl.pallas_call(
         separators,
         out_shape=(
             jax.ShapeDtypeStruct((leaves,) + block, BF16),
@@ -357,9 +374,9 @@
         in_specs=[smem, smem, smem, vmem, vmem, vmem, hbm, hbm],
         out_specs=(hbm, vmem, vmem),
         scratch_shapes=[
-            pltpu.VMEM((leaves, width, (slots + 1) * width), BF16),
+            pltpu.VMEM((leaves, slots, width, width), BF16),
+            pltpu.VMEM((leaves, width, slots * width), BF16),
             pltpu.VMEM((leaves,) + block, BF16),
-            pltpu.VMEM((LEAF_STEP,) + block, BF16),
             pltpu.VMEM((leaves,) + block, BF16),
             dma((2,)), dma((steps,)),
             pltpu.VMEM((chunks, 2 * fronts) + piece, BF16),
@@ -375,8 +392,23 @@
         ),
         cost_estimate=cost,
         name="separators",
-    )(rows, fill_count, panel_order, partial, sep_rhs, panel, turned, forward)
-    return (leaf_solution, sep_forward, sep_solution)
+    )(rows, fill_count, panel_order, partial, sep_rhs, panel, off_blocks, forward)
+
+    one_spec = pl.BlockSpec((1,) + block, lambda i: (0, 0, 0))
+    return pl.pallas_call(
+        leaf_finish,
+        grid=(steps,),
+        out_shape=(
+            jax.ShapeDtypeStruct((leaves,) + block, BF16),
+            jax.ShapeDtypeStruct((1,) + block, BF16),
+            jax.ShapeDtypeStruct((1,) + block, F32),
+        ),
+        in_specs=[inverse_spec, vector_spec, one_spec, one_spec],
+        out_specs=(vector_spec, one_spec, one_spec),
+        compiler_params=pltpu.CompilerParams(vmem_limit_bytes=VMEM_BYTES),
+        cost_estimate=cost,
+        name="leaf_finish",
+    )(leaf_inverse, backward, sep_forward, sep_solution)
 
 
 def solution(mesh):

time: 66.6 us -> 64.4 us (0.967)
  the two profiles are of different devices: /device:TPU:13 before, /device:TPU:0 now
where the time goes in v6:
time: 64.4 us; the launch traced here: 63.2 us
  Pallas kernels  62.5 us (97%)
    pallas_call x1, Pallas kernels, on_device(): pl.pallas_call(separators, out_shape=(jax.ShapeDtypeStruct((leaves,) + bl...  49.6 us
    pallas_call x1, Pallas kernels, on_device(): pl.pallas_call(leaf_forward, grid=(steps,), out_shape=(jax.ShapeDtypeStru...  8.3 us
    pallas_call x1, Pallas kernels, on_device(): pl.pallas_call(leaf_finish, grid=(steps,), out_shape=(jax.ShapeDtypeStruc...  4.62 us

profile of v6, /device:TPU:0, one launch (start us, length us, event | category | flops | bytes accessed | tf_op | source)
XLA Modules:
  0.0 63.2 jit_solution(12602551646832339434)
XLA Ops:
  0.6 8.3 %leaf_forward.1 = (bf16[32,128,256]{2,1,0:T(8,128)(2,1)}, bf16[2,16,128,128]{3,2,1,0:T(8,128)(2,1)}) custom-call(s32[5,32]{1,0:T(8,128)} %bitcast.3, s32[32]{0:T(128)} %fill_ref.3, bf16[32,128,128]{2,1,0:T(8,128)(2,1)} %inverse_ref.3, bf16[32,128,256]{2,1,0:T(8,128)(2,1)} %rhs_ref.2, bf16[32,5,128,128]{3,2,1,0:T(8,128)(2,1)} %off_hbm.1), custom_call_target="tpu_custom_call" | custom-call | flops 1610612736 | bytes 10485760 | tf_op jit(solution)/shard_map/leaf_forward/pallas_call | solution.py:346
  8.9 49.6 %separators.1 = (bf16[32,128,256]{2,1,0:T(8,128)(2,1)}, bf16[1,128,256]{2,1,0:T(8,128)(2,1)}, f32[1,128,256]{2,1,0:T(8,128)}) custom-call(s32[5,32]{1,0:T(8,128)} %bitcast.4, s32[32]{0:T(128)} %fill_ref.3, s32[1,8]{1,0:T(1,128)} %order_ref.1, bf16[2,16,128,128]{3,2,1,0:T(8,128)(2,1)} %get-tuple-element.8.partial_ref, bf16[1,128,256]{2,1,0:T(8,128)(2,1)} %rhs_ref.3, ...), custom_call_target="tpu_custom_call" | custom-call | flops 1610612736 | bytes 10485760 | tf_op jit(solution)/shard_map/separators/pallas_call | solution.py:367
  58.6 4.6 %leaf_finish.1 = (bf16[32,128,256]{2,1,0:T(8,128)(2,1)}, bf16[1,128,256]{2,1,0:T(8,128)(2,1)}, f32[1,128,256]{2,1,0:T(8,128)}) custom-call(bf16[32,128,128]{2,1,0:T(8,128)(2,1)} %inverse_ref.3, bf16[32,128,256]{2,1,0:T(8,128)(2,1)} %get-tuple-element.10.backward_ref, bf16[1,128,256]{2,1,0:T(8,128)(2,1)} %get-tuple-element.11.sep_fwd_ref, ...), custom_call_target="tpu_custom_call" | custom-call | flops 1610612736 | bytes 10485760 | tf_op jit(solution)/shard_map/leaf_finish/pallas_call | solution.py:398

commit v7 on v6

--- a/solution.py
+++ b/solution.py
@@ -162,8 +162,6 @@
             )
     for pp in parts:
         push(panel_ref, peer_panel.at[part], panel_send.at[pp], panel_recv.at[part], across(pp))
-    loads[0].wait()
-    turn(0)
     totals = []
     for ll in order:
         arrived(from_core.at[part, group(ll)], core_recv.at[part, ll])
@@ -180,7 +178,6 @@
                 to_z[f] = value.astype(BF16)
         if ll is not line:
             push(to_z.at[group(ll)], from_z.at[group(line)], z_send.at[ll], z_recv.at[line], along(ll))
-    turn(1)
     for ll in others:
         arrived(from_z.at[group(ll)], z_recv.at[ll])
         for k in range(chunks):
@@ -201,7 +198,9 @@
                 :, f * width : (f + 1) * width
             ].T
 
-    turn(2)
+    steps = leaf_out.shape[0] // LEAF_STEP
+    loads[0].wait()
+    turn(0, steps // 2)
     forward = [jnp.zeros((width, lanes), F32)] * chunks
     for ll in [line] + others:
         if ll is not line:
@@ -227,8 +226,7 @@
                 to_adjoint.at[group(ll)], from_adjoint.at[mine],
                 adj_send.at[ll], adj_recv.at[line], along(ll),
             )
-    steps = leaf_out.shape[0] // LEAF_STEP
-    turn(3, steps - 3)
+    turn(steps // 2, steps - steps // 2)
     for ll in others:
         arrived(from_adjoint.at[group(ll)], adj_recv.at[ll])
         solved += from_adjoint[group(ll)].reshape(chunks * width, lanes).astype(F32)

time: 64.4 us -> 64.6 us (level)
  the two profiles are of different devices: /device:TPU:0 before, /device:TPU:13 now
where the time goes in v7:
time: 64.6 us; the launch traced here: 64.3 us
  Pallas kernels  63.6 us (98%)
    pallas_call x1, Pallas kernels, on_device(): pl.pallas_call(separators, out_shape=(jax.ShapeDtypeStruct((leaves,) + bl...  50.7 us
    pallas_call x1, Pallas kernels, on_device(): pl.pallas_call(leaf_forward, grid=(steps,), out_shape=(jax.ShapeDtypeStru...  8.29 us
    pallas_call x1, Pallas kernels, on_device(): pl.pallas_call(leaf_finish, grid=(steps,), out_shape=(jax.ShapeDtypeStruc...  4.62 us

profile of v7, /device:TPU:13, one launch (start us, length us, event | category | flops | bytes accessed | tf_op | source)
XLA Modules:
  0.0 64.3 jit_solution(14653619667770643163)
XLA Ops:
  0.6 8.3 %leaf_forward.1 = (bf16[32,128,256]{2,1,0:T(8,128)(2,1)}, bf16[2,16,128,128]{3,2,1,0:T(8,128)(2,1)}) custom-call(s32[5,32]{1,0:T(8,128)} %bitcast.3, s32[32]{0:T(128)} %fill_ref.3, bf16[32,128,128]{2,1,0:T(8,128)(2,1)} %inverse_ref.3, bf16[32,128,256]{2,1,0:T(8,128)(2,1)} %rhs_ref.2, bf16[32,5,128,128]{3,2,1,0:T(8,128)(2,1)} %off_hbm.1), custom_call_target="tpu_custom_call" | custom-call | flops 1610612736 | bytes 10485760 | tf_op jit(solution)/shard_map/leaf_forward/pallas_call | solution.py:344
  8.9 50.7 %separators.1 = (bf16[32,128,256]{2,1,0:T(8,128)(2,1)}, bf16[1,128,256]{2,1,0:T(8,128)(2,1)}, f32[1,128,256]{2,1,0:T(8,128)}) custom-call(s32[5,32]{1,0:T(8,128)} %bitcast.4, s32[32]{0:T(128)} %fill_ref.3, s32[1,8]{1,0:T(1,128)} %order_ref.1, bf16[2,16,128,128]{3,2,1,0:T(8,128)(2,1)} %get-tuple-element.8.partial_ref, bf16[1,128,256]{2,1,0:T(8,128)(2,1)} %rhs_ref.3, ...), custom_call_target="tpu_custom_call" | custom-call | flops 1610612736 | bytes 10485760 | tf_op jit(solution)/shard_map/separators/pallas_call | solution.py:365
  59.7 4.6 %leaf_finish.1 = (bf16[32,128,256]{2,1,0:T(8,128)(2,1)}, bf16[1,128,256]{2,1,0:T(8,128)(2,1)}, f32[1,128,256]{2,1,0:T(8,128)}) custom-call(bf16[32,128,128]{2,1,0:T(8,128)(2,1)} %inverse_ref.3, bf16[32,128,256]{2,1,0:T(8,128)(2,1)} %get-tuple-element.10.backward_ref, bf16[1,128,256]{2,1,0:T(8,128)(2,1)} %get-tuple-element.11.sep_fwd_ref, ...), custom_call_target="tpu_custom_call" | custom-call | flops 1610612736 | bytes 10485760 | tf_op jit(solution)/shard_map/leaf_finish/pallas_call | solution.py:396
